TPU v7x, 512 devices: a whole 4x8x8 slice. The times are simulated.
512 devices in a mesh: stream: 64 (over z, y), head: 8 (over x, core).
Axes of the slice: x: 4, y: 8, z: 8, core: 2. Of those that a mesh axis runs over, the one named last changes fastest.
Arguments:
- queries: bfloat16 [64, 3, 8192], P('stream', None, 'head'), may hold values from -7 to 7
- new_kv: bfloat16 [64, 3, 2048], P('stream', None, 'head'), may hold values from -6 to 6
- cache_kv: bfloat16 [64, 2048, 2048], P('stream', None, 'head'), may hold values from -6 to 6
- cache_fill: int32 [64], P('stream'), may hold values from 1 to 2048, 65536 in all
- fresh_kv: bfloat16 [64, 1024, 2048], P(None, 'stream', 'head'), may hold values from -6 to 6
- fresh_len: int32 [64], replicated, may hold values from 1 to 1024, 32768 in all
- owner_slot: int32 [64], replicated, may hold values from 0 to 63, each once
- out_weight: bfloat16 [8192, 5120], P('head', 'stream'), may hold values from -0.0625 to 0.0625
Outputs:
- decoded: bfloat16 [64, 3, 5120], P(None, None, 'stream')
Inputs may be any that keep to these rules, and one draw needn't show every extreme that they name: `fresh_len`: one segment has exactly 1024 frames, every segment at least one.
All inputs are finite; a program needn't handle non-finite values. No bound on the sum of `cache_fill` on one device may be relied on, other than what follows from the above.
Results may differ from a plain program's by a relative error of at most 0.0055.
Values may be sent and summed in bfloat16 or wider, within the bound.
A program may use at most 64 MiB of HBM per device.

v0:
```python
import jax
import jax.numpy as jnp
from jax import lax
from jax.sharding import PartitionSpec as P

D_HEAD = 128
GROUP = 8
STEPS = 3
CBLK = 512


def split_pairs(packed, heads_here):
    shaped = packed.reshape(
        packed.shape[0], packed.shape[1], heads_here, 2, packed.shape[2] // (2 * heads_here)
    )
    return (shaped[:, :, :, 0], shaped[:, :, :, 1])


def block_pieces(query_matrix_rows, key_matrix_rows, value_rows, valid_mask, block_size):
    logit_scores = jnp.einsum(
        "xwve,xowe->xwvo", query_matrix_rows, key_matrix_rows, preferred_element_type=jnp.float32
    ) * query_matrix_rows.shape[-1] ** (-0.5)
    track_count, head_count, row_count, key_count = logit_scores.shape
    nblocks = key_count // block_size
    grouped = logit_scores.reshape(track_count, head_count, row_count, nblocks, block_size)
    allowed = jnp.broadcast_to(valid_mask, (track_count, 1, row_count, key_count)).reshape(
        track_count, 1, row_count, nblocks, block_size
    )
    highest = jnp.max(jnp.where(allowed, grouped, -1e30), axis=-1)
    weights = jnp.where(allowed, jnp.exp(grouped - highest[..., None]), 0.0)
    totals = jnp.sum(weights, axis=-1)
    values_grouped = value_rows.reshape(
        track_count, nblocks, block_size, head_count, value_rows.shape[-1]
    )
    outputs = jnp.einsum(
        "shrnb,snbhd->shrnd",
        weights.astype(jnp.bfloat16),
        values_grouped,
        preferred_element_type=jnp.float32,
    )
    return (highest, totals, outputs)


def combine_parts(portions):
    highest = jnp.concatenate([portion[0] for portion in portions], axis=3)
    totals = jnp.concatenate([portion[1] for portion in portions], axis=3)
    outputs = jnp.concatenate([portion[2] for portion in portions], axis=3)
    top_value = jnp.max(highest, axis=3, keepdims=True)
    factor = jnp.exp(highest - top_value)
    return (
        jnp.sum(factor[..., None] * outputs, axis=3) / jnp.sum(factor * totals, axis=3)[..., None]
    )


def shards(queries, new_kv, cache_kv, cache_fill, fresh_kv, fresh_len, owner_slot, out_weight):
    all_tracks = fresh_kv.shape[0]
    local_tracks = queries.shape[0]
    heads_here = new_kv.shape[2] // (2 * D_HEAD)
    row_count = STEPS * GROUP
    block_size = fresh_kv.shape[1]
    numbers = jnp.arange(all_tracks, dtype=jnp.int32)
    inverse_permutation_map = jnp.zeros((all_tracks,), jnp.int32).at[owner_slot].set(numbers)
    fresh_slot = fresh_kv[inverse_permutation_map]
    length_slot = fresh_len[inverse_permutation_map]
    own_slots = lax.axis_index("stream") * local_tracks + jnp.arange(local_tracks, dtype=jnp.int32)
    tracks_here = queries.shape[0]
    shaped = queries.reshape(tracks_here, STEPS, heads_here, GROUP, D_HEAD).transpose(0, 2, 1, 3, 4)
    query_matrix_rows = shaped.reshape(tracks_here, heads_here, row_count, D_HEAD)
    cache_keys, cache_values = split_pairs(cache_kv, heads_here)
    cache_span = cache_kv.shape[1]
    cache_valid = (jnp.arange(cache_span, dtype=jnp.int32)[None, :] < cache_fill[:, None]).reshape(
        local_tracks, 1, 1, cache_span
    )
    portions = [block_pieces(query_matrix_rows, cache_keys, cache_values, cache_valid, CBLK)]
    new_keys, new_values = split_pairs(new_kv, heads_here)
    step_of_row = jnp.arange(row_count, dtype=jnp.int32) // GROUP
    new_valid = (jnp.arange(STEPS, dtype=jnp.int32)[None, :] <= step_of_row[:, None]).reshape(
        1, 1, row_count, STEPS
    )
    portions.append(block_pieces(query_matrix_rows, new_keys, new_values, new_valid, STEPS))
    arrived = lax.all_to_all(fresh_slot, "stream", split_axis=0, concat_axis=1, tiled=True)
    fresh_keys, fresh_values = split_pairs(arrived, heads_here)
    fresh_span = arrived.shape[1]
    own_lengths = length_slot[own_slots]
    fresh_valid = (jnp.arange(fresh_span, dtype=jnp.int32)[None, :] < own_lengths[:, None]).reshape(
        local_tracks, 1, 1, fresh_span
    )
    portions.append(
        block_pieces(query_matrix_rows, fresh_keys, fresh_values, fresh_valid, block_size)
    )
    merged = combine_parts(portions)
    attention = merged.reshape(local_tracks, heads_here, STEPS, GROUP, D_HEAD).transpose(
        0, 2, 1, 3, 4
    )
    attention = attention.reshape(local_tracks * STEPS, heads_here * GROUP * D_HEAD).astype(
        jnp.bfloat16
    )
    partial_out = jnp.dot(
        lax.all_gather(attention, "stream", axis=0, tiled=True),
        out_weight,
        preferred_element_type=jnp.float32,
    )
    summed = lax.psum(partial_out, "head")
    decoded = summed.astype(jnp.bfloat16).reshape(all_tracks, STEPS, out_weight.shape[1])
    return decoded[owner_slot]


def solution(mesh):
    in_specs = (
        P("stream", None, "head"),
        P("stream", None, "head"),
        P("stream", None, "head"),
        P("stream"),
        P(None, "stream", "head"),
        P(),
        P(),
        P("head", "stream"),
    )
    out_specs = P(None, None, "stream")
    return jax.shard_map(shards, mesh=mesh, in_specs=in_specs, out_specs=out_specs, check_vma=False)
```

profile of v0, /device:TPU:1, one launch (start us, length us, event | category | flops | bytes accessed | tf_op | source)
XLA Modules:
  0.0 116.5 jit_solution(4449496020351502682)
XLA Ops:
  0.0 0.7 compare_select_fusion.1
  0.7 0.8 scatter_custom_fusion
  1.5 1.4 %gather_fusion.1 = bf16[64,16,256]{2,1,0:T(8,128)(2,1)} fusion(bf16[64,16,256]{2,1,0:T(8,128)(2,1)S(1)} %copy-done, s32[1024]{0:T(1024)S(1)} %pad_clamp_fusion.1), kind=kCustom, calls=%fused_computation.1 | custom fusion | bytes 1048832 | tf_op jit(solution)/shard_map/gather | solution.py:63
  2.9 17.3 %all-to-all-start = ((bf16[64,16,256]{2,1,0:T(8,128)(2,1)}), bf16[64,16,256]{2,1,0:T(8,128)(2,1)S(1)}, u32[]{:S(2)}, u32[]{:S(2)}) async-start(bf16[64,16,256]{2,1,0:T(8,128)(2,1)} %gather_fusion.1), calls=%async_computation | async-start | bytes 1048576 | tf_op jit(solution)/shard_map/all_to_all | solution.py:81
  20.9 0.0 copy-start.4
  20.9 0.8 gather_fusion
  21.7 0.6 dynamic-slice.2
  22.3 0.6 add_compare_fusion
  22.9 0.1 copy-done.5
  23.0 0.1 select_reduce_fusion.6
  23.1 0.1 lt.61
  23.2 0.1 copy.75
  23.3 0.1 copy.83
  23.4 0.1 copy.69
  23.5 0.1 copy.80
  23.6 0.6 copy.66
  24.3 0.3 copy.73
  24.6 0.3 select_reduce_fusion.3
  24.9 0.1 reshape.582
  25.0 0.1 select_reduce_fusion.4
  25.2 0.1 copy.71
  25.2 0.2 convolution_bitcast_fusion.2
  25.4 0.2 select_reduce_fusion.2
  25.7 0.2 convolution_bitcast_fusion.1
  25.9 11.4 %all-to-all-done = bf16[64,16,256]{2,1,0:T(8,128)(2,1)S(1)} async-done(((bf16[64,16,256]{2,1,0:T(8,128)(2,1)}), bf16[64,16,256]{2,1,0:T(8,128)(2,1)S(1)}, u32[]{:S(2)}, u32[]{:S(2)}) %all-to-all-start) | async-done | bytes 524320 | tf_op jit(solution)/shard_map/all_to_all | solution.py:81
  37.4 0.1 reshape.585
  37.5 0.7 fusion.27
  38.2 0.4 select_reduce_fusion.5
  38.6 0.3 reshape.587
  38.9 0.3 reshape.592
  39.2 0.3 select_reduce_fusion.1
  39.5 0.5 select_reduce_fusion
  40.0 0.2 copy.76
  40.3 0.3 copy.77
  40.6 0.1 fusion.11
  40.7 0.2 fusion.14
  40.9 0.1 div.25
  41.0 0.1 copy.70
  41.1 0.4 convolution_bitcast_fusion
  41.5 0.3 fusion.1
  41.9 36.3 %all-gather = bf16[64,3,1024]{2,1,0:T(4,128)(2,1)S(1)} all-gather(bf16[1,3,1024]{2,1,0:T(4,128)(2,1)S(1)} %fusion.15), channel_id=1, replica_groups=mesh['stream'=64,'head'=8] {'stream'}, dimensions={0}, use_global_device_ids=true | all-gather | bytes 399360 | tf_op jit(solution)/shard_map/all_gather | solution.py:99
  78.2 0.3 reshape.652
  78.5 0.6 copy-done.3
  79.1 0.3 fusion.28
  79.3 35.8 %psum.7 = bf16[192,80]{0,1:T(8,128)(2,1)S(1)} all-reduce(f32[192,80]{0,1:T(8,128)S(1)} %fusion.28), channel_id=1, replica_groups=mesh['stream'=64,'head'=8] {'head'}, use_global_device_ids=true, to_apply=%region_11.12 | all-reduce | flops 15360 | bytes 92160 | tf_op jit(solution)/shard_map/psum | solution.py:103
  115.1 0.1 copy.84
  115.3 0.7 gather_fusion.2
  115.9 0.6 copy.85
  (27 shorter events, 0.3 us)
Async XLA Ops:
  0.0 1.5 %copy-start = (bf16[64,16,256]{2,1,0:T(8,128)(2,1)S(1)}, bf16[64,16,256]{2,1,0:T(8,128)(2,1)}, u32[]{:S(2)}) copy-start(bf16[64,16,256]{2,1,0:T(8,128)(2,1)} %param.12) | copy-start | bytes 1572868
  2.9 20.7 %copy-start.2 = (bf16[1,2048,256]{2,1,0:T(8,128)(2,1)S(1)}, bf16[1,2048,256]{2,1,0:T(8,128)(2,1)}, u32[]{:S(2)}) copy-start(bf16[1,2048,256]{2,1,0:T(8,128)(2,1)} %param.10) | copy-start | bytes 3145732
  2.9 34.4 %all-to-all-start = ((bf16[64,16,256]{2,1,0:T(8,128)(2,1)}), bf16[64,16,256]{2,1,0:T(8,128)(2,1)S(1)}, u32[]{:S(2)}, u32[]{:S(2)}) async-start(bf16[64,16,256]{2,1,0:T(8,128)(2,1)} %gather_fusion.1), calls=%async_computation | async-start | bytes 1048576 | tf_op jit(solution)/shard_map/all_to_all | solution.py:81
  20.2 0.7 copy-start.1
  20.9 0.8 copy-start.4
  22.3 0.7 copy-start.5
  78.2 0.9 copy-start.3
where the time goes:
time: 118 us; the launch traced here: 117 us
  blocking collectives  72.1 us (61%)
  starting transfers between devices  17.3 us (15%)
  waiting for transfers between devices  11.4 us (10%)
  local copies, waits for them, and re-layouts  9.74 us (8%)
  other arithmetic  3.18 us (3%)
  matrix products  1.91 us (2%)
    all_gather x1, blocking collectives, shards(): lax.all_gather(attention, 'stream', axis=0, tiled=True)  36.3 us
    psum x1, blocking collectives, shards(): summed = lax.psum(partial_out, 'head')  35.8 us
    all_to_all x1, starting transfers between devices, shards(): lax.all_to_all(fresh_slot, 'stream', split_axis=0, concat_axis=1, tiled=T...  17.3 us
    all_to_all x1, waiting for transfers between devices, shards(): lax.all_to_all(fresh_slot, 'stream', split_axis=0, concat_axis=1, tiled=T...  11.4 us
  transfers between devices with their start and end apart: 1, of which 1 were waited for; matrix products, arithmetic and copies ran while one was open for 4% of the time, Pallas kernels for 0%

commit v1 on v0

v1 whole, which is shorter than its diff:
```python
import functools

import jax
import jax.numpy as jnp
from jax import lax
from jax.experimental import pallas as pl
from jax.experimental.pallas import tpu as pltpu
from jax.sharding import PartitionSpec as P

D_HEAD = 128
GROUP = 8
STEPS = 3
ROWS = STEPS * GROUP
PAD = 32
CBLK = 512
SIDE = 8
HALF = 4
NONE = -1e30
SCALE = D_HEAD**-0.5
FAR_FIRST = (4, 3, 5, 2, 6, 1, 7)
MESH = pl.DeviceIdType.MESH


def remote(src, dst, send_sem, recv_sem, device):
    return pltpu.make_async_remote_copy(
        src_ref=src,
        dst_ref=dst,
        send_sem=send_sem,
        recv_sem=recv_sem,
        device_id=device,
        device_id_type=MESH,
    )


def attend(query_rows, keys, values, valid):
    scores = (
        lax.dot_general(
            query_rows, keys, (((1,), (1,)), ((), ())), preferred_element_type=jnp.float32
        )
        * SCALE
    )
    highest = jnp.max(jnp.where(valid, scores, NONE), axis=1, keepdims=True)
    weights = jnp.where(valid, jnp.exp(scores - highest), 0.0)
    total = jnp.sum(weights, axis=1, keepdims=True)
    output = jnp.dot(weights.astype(jnp.bfloat16), values, preferred_element_type=jnp.float32)
    return highest, total, output


def merge(parts):
    top = functools.reduce(jnp.maximum, [part[0] for part in parts])
    factors = [jnp.exp(part[0] - top) for part in parts]
    total = sum(f * part[1] for f, part in zip(factors, parts))
    output = sum(f * part[2] for f, part in zip(factors, parts))
    return top, total, output


def kernel(
    owner_row_ref,
    owner_ref,
    len_ref,
    fill_ref,
    query_ref,
    new_ref,
    cache_hbm,
    fresh_hbm,
    weight_hbm,
    out_ref,
    cache,
    fresh,
    weight,
    table,
    table_smem,
    query_f32,
    query_all,
    send_kv,
    recv_kv,
    state_m,
    state_l,
    state_o,
    pieces,
    gathered,
    stage,
    ordered,
    partial,
    from_core,
    from_x,
    final,
    local_sem,
    q_send,
    q_recv,
    kv_send,
    kv_recv,
    o_send,
    o_recv,
    g_send,
    g_recv,
    c_send,
    c_recv,
    x_send,
    x_recv,
):
    stream = lax.axis_index("stream")
    head = lax.axis_index("head")
    z, y = stream // SIDE, stream % SIDE
    x, core = head // 2, head % 2
    me = (z, y)

    def at(zz, yy):
        return {"stream": lax.rem(zz, SIDE) * SIDE + lax.rem(yy, SIDE)}

    def along(axis, step):
        return at(z + step, y) if axis == 0 else at(z, y + step)

    def x_peer(step):
        return {"head": lax.rem(x + step, 4) * 2 + core}

    other_core = {"head": x * 2 + 1 - core}

    barrier = pltpu.get_barrier_semaphore()
    peers = [along(axis, step) for step in FAR_FIRST for axis in (0, 1)]
    peers += [x_peer(step) for step in (2, 1, 3)] + [other_core]
    for peer in peers:
        pl.semaphore_signal(barrier, inc=1, device_id=peer, device_id_type=MESH)

    load_fresh = pltpu.make_async_copy(fresh_hbm, fresh, local_sem.at[0])
    load_cache = pltpu.make_async_copy(cache_hbm, cache, local_sem.at[1])
    load_weight = pltpu.make_async_copy(weight_hbm, weight, local_sem.at[2])
    load_fresh.start()
    load_cache.start()
    load_weight.start()

    n_tracks = owner_row_ref.shape[1]
    owner = owner_row_ref[...]
    slot_of = lax.broadcasted_iota(jnp.int32, (n_tracks, n_tracks), 0)
    lane_of = lax.broadcasted_iota(jnp.int32, (n_tracks, n_tracks), 1)
    track_column = jnp.max(jnp.where(owner == slot_of, lane_of, 0), axis=1, keepdims=True)
    track_row = jnp.max(jnp.where(slot_of == lane_of, track_column, 0), axis=0, keepdims=True)
    owner_z, owner_y = owner // SIDE, owner % SIDE
    place_row = jnp.where(
        (owner_z + owner_y) % 2 == 0,
        owner_z * HALF + owner_y // 2,
        SIDE * HALF + owner_y * HALF + owner_z // 2,
    )
    table[...] = jnp.zeros_like(table)
    table[0:1, 0:n_tracks] = track_row
    table[1:2, 0:n_tracks] = place_row
    load_table = pltpu.make_async_copy(table, table_smem, local_sem.at[3])
    load_table.start()

    query_f32[...] = jnp.zeros_like(query_f32)
    query_flat = query_ref[0].astype(jnp.float32)
    for g in range(GROUP):
        query_f32[pl.ds(g, STEPS, stride=GROUP), :] = query_flat[
            :, g * D_HEAD : (g + 1) * D_HEAD
        ]
    parity = (z + y) % 2
    mine = jnp.where(parity == 0, y // 2, HALF + z // 2)
    my_query = query_f32[...].astype(jnp.bfloat16)
    query_all[mine] = my_query
    state_m[...] = jnp.full_like(state_m, NONE)
    state_l[...] = jnp.zeros_like(state_l)
    state_o[...] = jnp.zeros_like(state_o)
    partial[...] = jnp.zeros_like(partial)

    load_table.wait()
    load_fresh.wait()

    def slot_at(kind, place, i):
        if kind == 0:
            return place * SIDE + 2 * i + place % 2
        return (2 * i + 1 - place % 2) * SIDE + place

    for kind in (0, 1):
        for place in range(SIDE):
            for i in range(HALF):
                send_kv[kind, place, i] = fresh[table_smem[0, slot_at(kind, place, i)]]
    for kind in (0, 1):
        recv_kv[kind, me[kind]] = send_kv[kind, me[kind]]

    pl.semaphore_wait(barrier, len(peers))

    q_copies = []
    for n, step in enumerate(FAR_FIRST):
        peer = at(z + step * parity, y + step * (1 - parity))
        q_copies.append(
            remote(query_all.at[mine], query_all.at[mine], q_send.at[n], q_recv.at[mine], peer)
        )
        q_copies[-1].start()
    kv_copies = []
    for n, step in enumerate(FAR_FIRST):
        for kind in (0, 1):
            there = lax.rem(me[kind] + step, SIDE)
            kv_copies.append(
                remote(
                    send_kv.at[kind, there],
                    recv_kv.at[kind, me[kind]],
                    kv_send.at[kind, n],
                    kv_recv.at[kind, me[kind]],
                    along(kind, step),
                )
            )
            kv_copies[-1].start()

    load_cache.wait()
    parts = []
    fill = fill_ref[0]
    for block in range(cache.shape[0] // CBLK):
        rows = pl.ds(block * CBLK, CBLK)
        position = block * CBLK + lax.broadcasted_iota(jnp.int32, (PAD, CBLK), 1)
        parts.append(
            attend(my_query, cache[rows, :D_HEAD], cache[rows, D_HEAD:], position < fill)
        )
    query_full = query_f32[...]
    new_rows = new_ref[0].astype(jnp.float32)
    step_of_row = lax.broadcasted_iota(jnp.int32, (PAD, 1), 0) // GROUP
    new_scores = [
        jnp.where(
            u <= step_of_row,
            jnp.sum(query_full * new_rows[u : u + 1, :D_HEAD], axis=1, keepdims=True) * SCALE,
            NONE,
        )
        for u in range(STEPS)
    ]
    new_top = functools.reduce(jnp.maximum, new_scores)
    new_weights = [
        jnp.where(u <= step_of_row, jnp.exp(new_scores[u] - new_top), 0.0) for u in range(STEPS)
    ]
    new_output = sum(
        new_weights[u].astype(jnp.bfloat16).astype(jnp.float32) * new_rows[u : u + 1, D_HEAD:]
        for u in range(STEPS)
    )
    parts.append((new_top, sum(new_weights), new_output))
    top, total, output = merge(parts)
    state_m[mine] = jnp.broadcast_to(top, (PAD, D_HEAD))
    state_l[mine] = jnp.broadcast_to(total, (PAD, D_HEAD))
    state_o[mine] = output

    index_of_mine = lax.rem(mine, HALF)
    for n in range(2 * HALF - 1):
        if n < HALF - 1:
            came = parity * HALF + lax.rem(index_of_mine + 1 + n, HALF)
        else:
            came = (1 - parity) * HALF + n - (HALF - 1)
        remote(
            query_all.at[came], query_all.at[came], q_send.at[n], q_recv.at[came], other_core
        ).wait_recv()
    for step in FAR_FIRST[::-1]:
        for kind in (0, 1):
            there = lax.rem(me[kind] + step, SIDE)
            remote(
                send_kv.at[kind, there],
                recv_kv.at[kind, there],
                kv_send.at[kind, 0],
                kv_recv.at[kind, there],
                other_core,
            ).wait_recv()

    span = SIDE * 16
    lane = lax.broadcasted_iota(jnp.int32, (1, span), 1)
    positions = ((lane // 16) * SIDE * 16 + y * 16 + lane % 16, z * span + lane)
    row_id = lax.broadcasted_iota(jnp.int32, (PAD, D_HEAD), 0)
    lane_id = lax.broadcasted_iota(jnp.int32, (PAD, D_HEAD), 1)
    diagonal = row_id == lane_id
    row8 = lax.broadcasted_iota(jnp.int32, (8, D_HEAD), 0)
    for kind in (0, 1):
        for i in range(HALF):
            n = kind * HALF + i
            if kind == 0:
                slot = z * SIDE + 2 * i + z % 2
            else:
                slot = (2 * i + 1 - y % 2) * SIDE + y
            length = len_ref[table_smem[0, slot]]
            keys = recv_kv[kind, :, i, :, :D_HEAD].reshape(span, D_HEAD)
            values = recv_kv[kind, :, i, :, D_HEAD:].reshape(span, D_HEAD)
            top, total, output = merge(
                [
                    attend(query_all[n], keys, values, positions[kind] < length),
                    (state_m[n], state_l[n], state_o[n]),
                ]
            )
            log_sum = top + jnp.log(jnp.maximum(total, 0.5))
            output = output / jnp.maximum(total, 0.5)
            line = jnp.sum(jnp.where(diagonal, log_sum, 0.0), axis=0, keepdims=True)
            first = line.astype(jnp.bfloat16).astype(jnp.float32)
            second = (line - first).astype(jnp.bfloat16).astype(jnp.float32)
            third = line - first - second
            lines = jnp.where(
                row8 == 0,
                first,
                jnp.where(row8 == 1, second, jnp.where(row8 == 2, third, 0.0)),
            )
            pieces[kind, me[1 - kind], i] = jnp.concatenate(
                [output[:ROWS], lines], axis=0
            ).astype(jnp.bfloat16)

    o_copies = []
    for n, step in enumerate(FAR_FIRST):
        for kind in (0, 1):
            mine_here = me[1 - kind]
            o_copies.append(
                remote(
                    pieces.at[kind, mine_here],
                    pieces.at[kind, mine_here],
                    o_send.at[kind, n],
                    o_recv.at[kind, mine_here],
                    along(1 - kind, step),
                )
            )
            o_copies[-1].start()
    for step in FAR_FIRST[::-1]:
        for kind in (0, 1):
            there = lax.rem(me[1 - kind] + step, SIDE)
            remote(
                pieces.at[kind, there],
                pieces.at[kind, there],
                o_send.at[kind, 0],
                o_recv.at[kind, there],
                other_core,
            ).wait_recv()

    for kind in (0, 1):
        rows = []
        for i in range(HALF):
            arrived = [pieces[kind, src, i].astype(jnp.float32) for src in range(SIDE)]
            logs = [jnp.sum(a[ROWS:], axis=0, keepdims=True) for a in arrived]
            top = functools.reduce(jnp.maximum, logs)
            shares = [jnp.exp(log - top) for log in logs]
            total = sum(shares)
            acc = None
            for a, share in zip(arrived, shares):
                column = jnp.sum(
                    jnp.where(diagonal[:ROWS], share / total, 0.0), axis=1, keepdims=True
                )
                term = column * a[:ROWS]
                acc = term if acc is None else acc + term
            rows.append(acc)
        gathered[kind, me[kind]] = jnp.concatenate(rows, axis=0).astype(jnp.bfloat16)

    g_copies = []
    for n, step in enumerate(FAR_FIRST):
        for kind in (0, 1):
            g_copies.append(
                remote(
                    gathered.at[kind, me[kind]],
                    gathered.at[kind, me[kind]],
                    g_send.at[kind, n],
                    g_recv.at[kind, me[kind]],
                    along(kind, step),
                )
            )
            g_copies[-1].start()
    load_weight.wait()
    for step in (0,) + FAR_FIRST[::-1]:
        for kind in (0, 1):
            there = lax.rem(me[kind] + step, SIDE)
            if step:
                remote(
                    gathered.at[kind, there],
                    gathered.at[kind, there],
                    g_send.at[kind, 0],
                    g_recv.at[kind, there],
                    other_core,
                ).wait_recv()
            stage[pl.ds((kind * SIDE + there) * HALF, HALF)] = (
                gathered[kind, there].astype(jnp.float32).reshape(HALF, ROWS, D_HEAD)
            )

    for track in range(n_tracks):
        rows = stage[table_smem[1, track]]
        for t in range(STEPS):
            ordered[pl.ds((t * n_tracks + track) * GROUP, GROUP), :] = rows[
                t * GROUP : (t + 1) * GROUP
            ]
    width = weight.shape[0]
    product = None
    for g in range(GROUP):
        left = ordered[pl.ds(g, n_tracks * STEPS, stride=GROUP), :].astype(jnp.bfloat16)
        term = lax.dot_general(
            left,
            weight[:, g * D_HEAD : (g + 1) * D_HEAD],
            (((1,), (1,)), ((), ())),
            preferred_element_type=jnp.float32,
        )
        product = term if product is None else product + term
    half = n_tracks * STEPS // 2
    partial[0, :, :width] = product[:half]
    partial[1, :, :width] = product[half:]

    swap = remote(
        partial.at[1 - core], from_core, c_send.at[0], c_recv.at[0], other_core
    )
    swap.start()
    swap.wait_recv()
    from_x[x] = (partial[core] + from_core[...]).astype(jnp.bfloat16)
    x_copies = []
    for n, step in enumerate((2, 1, 3)):
        x_copies.append(
            remote(from_x.at[x], from_x.at[x], x_send.at[n], x_recv.at[x], x_peer(step))
        )
        x_copies[-1].start()
    for step in (1, 3, 2):
        there = lax.rem(x + step, 4)
        remote(
            from_x.at[there], from_x.at[there], x_send.at[0], x_recv.at[there], other_core
        ).wait_recv()
    summed = from_x[0].astype(jnp.float32)
    for there in range(1, 4):
        summed = summed + from_x[there].astype(jnp.float32)
    final[core] = summed.astype(jnp.bfloat16)
    give = remote(final.at[core], final.at[core], c_send.at[1], c_recv.at[1 + core], other_core)
    give.start()
    remote(
        final.at[1 - core], final.at[1 - core], c_send.at[1], c_recv.at[2 - core], other_core
    ).wait_recv()
    out_ref[0:half] = final[0][:, :width]
    out_ref[half:] = final[1][:, :width]

    for copy in q_copies + kv_copies + o_copies + g_copies + [swap] + x_copies + [give]:
        copy.wait_send()


def shards(queries, new_kv, cache_kv, cache_fill, fresh_kv, fresh_len, owner_slot, out_weight):
    n_tracks, depth = fresh_kv.shape[0], fresh_kv.shape[1]
    width = out_weight.shape[1]
    half = n_tracks * STEPS // 2
    vmem = pl.BlockSpec(memory_space=pltpu.VMEM)
    smem = pl.BlockSpec(memory_space=pltpu.SMEM)
    anywhere = pl.BlockSpec(memory_space=pl.ANY)
    bf16, f32 = jnp.bfloat16, jnp.float32
    dma = pltpu.SemaphoreType.DMA
    out = pl.pallas_call(
        kernel,
        name="handoff_decode",
        out_shape=jax.ShapeDtypeStruct((n_tracks * STEPS, width), bf16),
        in_specs=[vmem, smem, smem, smem, vmem, vmem, anywhere, anywhere, anywhere],
        out_specs=vmem,
        scratch_shapes=[
            pltpu.VMEM(cache_kv.shape[1:], bf16),
            pltpu.VMEM(fresh_kv.shape, bf16),
            pltpu.VMEM(out_weight.shape[::-1], bf16),
            pltpu.VMEM((8, 128), jnp.int32),
            pltpu.SMEM((8, 128), jnp.int32),
            pltpu.VMEM((PAD, D_HEAD), f32),
            pltpu.VMEM((2 * HALF, PAD, D_HEAD), bf16),
            pltpu.VMEM((2, SIDE, HALF, depth, 2 * D_HEAD), bf16),
            pltpu.VMEM((2, SIDE, HALF, depth, 2 * D_HEAD), bf16),
            pltpu.VMEM((2 * HALF, PAD, D_HEAD), f32),
            pltpu.VMEM((2 * HALF, PAD, D_HEAD), f32),
            pltpu.VMEM((2 * HALF, PAD, D_HEAD), f32),
            pltpu.VMEM((2, SIDE, HALF, PAD, D_HEAD), bf16),
            pltpu.VMEM((2, SIDE, HALF * ROWS, D_HEAD), bf16),
            pltpu.VMEM((n_tracks, ROWS, D_HEAD), f32),
            pltpu.VMEM((n_tracks * ROWS, D_HEAD), f32),
            pltpu.VMEM((2, half, 128), f32),
            pltpu.VMEM((half, 128), f32),
            pltpu.VMEM((4, half, 128), bf16),
            pltpu.VMEM((2, half, 128), bf16),
            dma((4,)),
            dma((SIDE - 1,)),
            dma((2 * HALF,)),
            dma((2, SIDE - 1)),
            dma((2, SIDE)),
            dma((2, SIDE - 1)),
            dma((2, SIDE)),
            dma((2, SIDE - 1)),
            dma((2, SIDE)),
            dma((2,)),
            dma((3,)),
            dma((3,)),
            dma((4,)),
        ],
        compiler_params=pltpu.CompilerParams(
            collective_id=0, has_side_effects=True, vmem_limit_bytes=32 * 1024 * 1024
        ),
    )(
        owner_slot[None, :],
        owner_slot,
        fresh_len,
        cache_fill,
        queries,
        new_kv,
        cache_kv[0],
        fresh_kv,
        out_weight.T,
    )
    return out.reshape(STEPS, n_tracks, width).transpose(1, 0, 2)


def solution(mesh):
    in_specs = (
        P("stream", None, "head"),
        P("stream", None, "head"),
        P("stream", None, "head"),
        P("stream"),
        P(None, "stream", "head"),
        P(),
        P(),
        P("head", "stream"),
    )
    out_specs = P(None, None, "stream")
    return jax.shard_map(shards, mesh=mesh, in_specs=in_specs, out_specs=out_specs, check_vma=False)
```

time: 118 us -> 55 us (0.47); the launches traced: 117 us -> 54.7 us
  blocking collectives: 72.1 us -> 0 us
  Pallas kernels: 0 us -> 48.9 us
  starting transfers between devices: 17.3 us -> 0 us
  waiting for transfers between devices: 11.4 us -> 0 us
  local copies, waits for them, and re-layouts: 9.74 us -> 5.16 us
  other arithmetic: 3.18 us -> 0 us
  matrix products: 1.91 us -> 0 us
    pallas_call x0 -> x1, Pallas kernels: none -> 48.9 us  [shards(): pl.pallas_call(kernel, name='handoff_decode', out_shape=jax.ShapeDtypeStr...]
    all_gather x1 -> x0, blocking collectives: 36.3 us -> none  [shards(): lax.all_gather(attention, 'stream', axis=0, tiled=True)]
    psum x1 -> x0, blocking collectives: 35.8 us -> none  [shards(): summed = lax.psum(partial_out, 'head')]
    all_to_all x1 -> x0, starting transfers between devices: 17.3 us -> none  [shards(): lax.all_to_all(fresh_slot, 'stream', split_axis=0, concat_axis=1, tiled=T...]
    all_to_all x1 -> x0, waiting for transfers between devices: 11.4 us -> none  [shards(): lax.all_to_all(fresh_slot, 'stream', split_axis=0, concat_axis=1, tiled=T...]
    gather x5 -> x0, local copies, waits for them, and re-layouts: 4.02 us -> none  [the longest x1 1.38 us: shards(): fresh_slot = fresh_kv[inverse_permutation_map]]
    unnamed x16 -> x15, local copies, waits for them, and re-layouts: 1.7 us -> 5.16 us
    dot_general x7 -> x0, matrix products: 1.91 us -> none  [the longest x3 0.86 us: block_pieces(): jnp.einsum('shrnb,snbhd->shrnd', weights.astype(jnp.bfloat16), values_gro...]
  transfers between devices with their start and end apart: 1 -> 0, of which waited for: 1 -> 0; matrix products, arithmetic and copies ran while one was open for 4% -> 0% of each run, Pallas kernels for 0% -> 0%
where the time goes in v1:
time: 55 us; the launch traced here: 54.7 us
  Pallas kernels  48.9 us (89%)
  local copies, waits for them, and re-layouts  5.16 us (9%)
  between operations  0.69 us (1%)
    pallas_call x1, Pallas kernels, shards(): pl.pallas_call(kernel, name='handoff_decode', out_shape=jax.ShapeDtypeStr...  48.9 us
    unnamed x15, local copies, waits for them, and re-layouts  5.16 us

profile of v1, /device:TPU:1, one launch (start us, length us, event | category | flops | bytes accessed | tf_op | source)
XLA Modules:
  0.0 54.7 jit_solution(4969907641532826378)
XLA Ops:
  0.7 0.0 copy-start.4
  0.7 0.0 copy-start.5
  0.7 0.0 copy-start.6
  0.7 0.7 %copy-done.4 = bf16[1,3,256]{2,1,0:T(4,128)(2,1)S(1)} copy-done((bf16[1,3,256]{2,1,0:T(4,128)(2,1)S(1)}, bf16[1,3,256]{2,1,0:T(4,128)(2,1)}, u32[]{:S(2)}) %copy-start.4) | copy-done | bytes 1560
  1.3 0.0 copy-done.5
  1.3 0.0 copy-done.6
  1.3 0.0 copy-start
  1.3 1.2 %copy-done = bf16[1,2048,256]{2,1,0:T(8,128)(2,1)S(1)} copy-done((bf16[1,2048,256]{2,1,0:T(8,128)(2,1)S(1)}, bf16[1,2048,256]{2,1,0:T(8,128)(2,1)}, u32[]{:S(2)}) %copy-start) | copy-done | bytes 1048600
  2.6 0.0 copy-start.1
  2.6 1.0 %copy-done.1 = bf16[64,16,256]{2,1,0:T(8,128)(2,1)S(1)} copy-done((bf16[64,16,256]{2,1,0:T(8,128)(2,1)S(1)}, bf16[64,16,256]{2,1,0:T(8,128)(2,1)}, u32[]{:S(2)}) %copy-start.1) | copy-done | bytes 524312
  3.6 0.0 copy-start.2
  3.6 0.9 %copy-done.2 = bf16[1024,80]{0,1:T(8,128)(2,1)S(1)} copy-done((bf16[1024,80]{0,1:T(8,128)(2,1)S(1)}, bf16[1024,80]{0,1:T(8,128)(2,1)}, u32[]{:S(2)}) %copy-start.2) | copy-done | bytes 163864
  4.5 0.0 copy-start.3
  4.5 0.7 %copy-done.3 = bf16[1,3,1024]{2,1,0:T(4,128)(2,1)S(1)} copy-done((bf16[1,3,1024]{2,1,0:T(4,128)(2,1)S(1)}, bf16[1,3,1024]{2,1,0:T(4,128)(2,1)}, u32[]{:S(2)}) %copy-start.3) | copy-done | bytes 6168
  5.2 48.9 %handoff_decode.1 = bf16[192,80]{1,0:T(8,128)(2,1)S(1)} custom-call(s32[1,64]{1,0:T(1,128)S(1)} %bitcast.9, s32[64]{0:T(128)S(1)} %copy-done.5, s32[64]{0:T(128)S(1)} %copy-done.6, s32[1]{0:T(128)S(6)} %copy.10.fill_ref, bf16[1,3,1024]{2,1,0:T(4,128)(2,1)S(1)} %copy-done.3, bf16[1,3,256]{2,1,0:T(4,128)(2,1)S(1)} %copy-done.4, bf16[2048,256]{1,0:T(8,128)(2,1)S(1)} %bitcast.6, ...), custom_call_target="tpu_custom_call" | custom-call | tf_op jit(solution)/shard_map/handoff_decode/pallas_call | solution.py:431
  54.1 0.6 %copy.11 = bf16[64,3,80]{2,0,1:T(8,128)(2,1)} copy(bf16[64,3,80]{2,0,1:T(8,128)(2,1)S(1)} %bitcast.7) | data formatting | bytes 61440
Async XLA Ops:
  0.7 0.7 %copy-start.4 = (bf16[1,3,256]{2,1,0:T(4,128)(2,1)S(1)}, bf16[1,3,256]{2,1,0:T(4,128)(2,1)}, u32[]{:S(2)}) copy-start(bf16[1,3,256]{2,1,0:T(4,128)(2,1)} %new_ref.1) | copy-start | bytes 4612
  0.7 0.7 %copy-start.5 = (s32[64]{0:T(128)S(1)}, s32[64]{0:T(128)}, u32[]{:S(2)}) copy-start(s32[64]{0:T(128)} %owner_ref.1) | copy-start | bytes 772
  0.7 0.7 %copy-start.6 = (s32[64]{0:T(128)S(1)}, s32[64]{0:T(128)}, u32[]{:S(2)}) copy-start(s32[64]{0:T(128)} %len_ref.1) | copy-start | bytes 772
  1.3 1.2 %copy-start = (bf16[1,2048,256]{2,1,0:T(8,128)(2,1)S(1)}, bf16[1,2048,256]{2,1,0:T(8,128)(2,1)}, u32[]{:S(2)}) copy-start(bf16[1,2048,256]{2,1,0:T(8,128)(2,1)} %param.10) | copy-start | bytes 3145732
  2.6 1.0 %copy-start.1 = (bf16[64,16,256]{2,1,0:T(8,128)(2,1)S(1)}, bf16[64,16,256]{2,1,0:T(8,128)(2,1)}, u32[]{:S(2)}) copy-start(bf16[64,16,256]{2,1,0:T(8,128)(2,1)} %fresh_hbm.1) | copy-start | bytes 1572868
  3.6 0.9 %copy-start.2 = (bf16[1024,80]{0,1:T(8,128)(2,1)S(1)}, bf16[1024,80]{0,1:T(8,128)(2,1)}, u32[]{:S(2)}) copy-start(bf16[1024,80]{0,1:T(8,128)(2,1)} %param.15) | copy-start | bytes 491524
  4.5 0.7 %copy-start.3 = (bf16[1,3,1024]{2,1,0:T(4,128)(2,1)S(1)}, bf16[1,3,1024]{2,1,0:T(4,128)(2,1)}, u32[]{:S(2)}) copy-start(bf16[1,3,1024]{2,1,0:T(4,128)(2,1)} %query_ref.1) | copy-start | bytes 18436

commit v2 on v1

v2 whole, which is shorter than its diff:
```python
import functools

import jax
import jax.numpy as jnp
from jax import lax
from jax.experimental import pallas as pl
from jax.experimental.pallas import tpu as pltpu
from jax.sharding import PartitionSpec as P

D_HEAD = 128
GROUP = 8
STEPS = 3
ROWS = STEPS * GROUP
PAD = 32
CBLK = 512
SIDE = 8
HALF = 4
BAND = HALF * ROWS
PIECE = BAND + 16
NONE = -1e30
SCALE = D_HEAD**-0.5
FAR_FIRST = (4, 3, 5, 2, 6, 1, 7)
HEAD_ORDER = (4, 5, 2, 3, 6, 7, 1)
MESH = pl.DeviceIdType.MESH


def remote(src, dst, send_sem, recv_sem, device):
    return pltpu.make_async_remote_copy(
        src_ref=src,
        dst_ref=dst,
        send_sem=send_sem,
        recv_sem=recv_sem,
        device_id=device,
        device_id_type=MESH,
    )


def attend(query_rows, keys, values, valid):
    scores = (
        lax.dot_general(
            query_rows, keys, (((1,), (1,)), ((), ())), preferred_element_type=jnp.float32
        )
        * SCALE
    )
    highest = jnp.max(jnp.where(valid, scores, NONE), axis=1, keepdims=True)
    weights = jnp.where(valid, jnp.exp(scores - highest), 0.0)
    total = jnp.sum(weights, axis=1, keepdims=True)
    output = jnp.dot(weights.astype(jnp.bfloat16), values, preferred_element_type=jnp.float32)
    return highest, total, output


def merge(parts):
    top = functools.reduce(jnp.maximum, [part[0] for part in parts])
    factors = [jnp.exp(part[0] - top) for part in parts]
    total = sum(f * part[1] for f, part in zip(factors, parts))
    output = sum(f * part[2] for f, part in zip(factors, parts))
    return top, total, output


def kernel(
    fill_ref,
    owner_hbm,
    len_hbm,
    query_hbm,
    new_hbm,
    cache_hbm,
    fresh_hbm,
    weight_hbm,
    out_ref,
    owner_row_ref,
    len_ref,
    query_ref,
    new_ref,
    cache,
    fresh,
    weight,
    table,
    table_smem,
    query_f32,
    query_all,
    send_kv,
    recv_kv,
    cache_out,
    cache_log,
    pieces,
    gathered,
    stage,
    ordered,
    sums,
    local_sem,
    q_send,
    q_recv,
    kv_send,
    kv_recv,
    o_send,
    o_recv,
    g_send,
    g_recv,
    s_send,
    s_recv,
):
    stream = lax.axis_index("stream")
    head = lax.axis_index("head")
    z, y = stream // SIDE, stream % SIDE
    n_heads = 8
    me = (z, y)

    def at(zz, yy):
        return {"stream": lax.rem(zz, SIDE) * SIDE + lax.rem(yy, SIDE)}

    def along(axis, step):
        return at(z + step, y) if axis == 0 else at(z, y + step)

    def head_peer(step):
        return {"head": lax.rem(head + step, n_heads)}

    any_peer = head_peer(1)

    load_owner = pltpu.make_async_copy(owner_hbm, owner_row_ref, local_sem.at[0])
    load_owner.start()
    barrier = pltpu.get_barrier_semaphore()
    peers = [along(axis, step) for step in FAR_FIRST for axis in (0, 1)]
    peers += [head_peer(step) for step in range(1, n_heads)]
    for peer in peers:
        pl.semaphore_signal(barrier, inc=1, device_id=peer, device_id_type=MESH)

    loads = [
        pltpu.make_async_copy(src, dst, local_sem.at[1 + n])
        for n, (src, dst) in enumerate(
            (
                (fresh_hbm, fresh),
                (query_hbm, query_ref),
                (new_hbm, new_ref),
                (cache_hbm, cache),
                (len_hbm, len_ref),
                (weight_hbm, weight.at[pl.ds(0, weight_hbm.shape[0])]),
            )
        )
    ]
    for load in loads:
        load.start()
    load_fresh, load_query, load_new, load_cache, load_len, load_weight = loads

    n_tracks = owner_row_ref.shape[1]
    load_owner.wait()
    owner = owner_row_ref[...]
    slot_of = lax.broadcasted_iota(jnp.int32, (n_tracks, n_tracks), 0)
    lane_of = lax.broadcasted_iota(jnp.int32, (n_tracks, n_tracks), 1)
    track_column = jnp.max(jnp.where(owner == slot_of, lane_of, 0), axis=1, keepdims=True)
    track_row = jnp.max(jnp.where(slot_of == lane_of, track_column, 0), axis=0, keepdims=True)
    owner_z, owner_y = owner // SIDE, owner % SIDE
    place_row = jnp.where(
        (owner_z + owner_y) % 2 == 0,
        owner_z * HALF + owner_y // 2,
        SIDE * HALF + owner_y * HALF + owner_z // 2,
    )
    table[...] = jnp.zeros_like(table)
    table[0:1, 0:n_tracks] = track_row
    table[1:2, 0:n_tracks] = place_row
    load_table = pltpu.make_async_copy(table, table_smem, local_sem.at[7])
    load_table.start()

    query_f32[...] = jnp.zeros_like(query_f32)
    load_query.wait()
    query_flat = query_ref[0].astype(jnp.float32)
    for g in range(GROUP):
        query_f32[pl.ds(g, STEPS, stride=GROUP), :] = query_flat[
            :, g * D_HEAD : (g + 1) * D_HEAD
        ]
    parity = (z + y) % 2
    mine = jnp.where(parity == 0, y // 2, HALF + z // 2)
    my_query = query_f32[...].astype(jnp.bfloat16)
    query_all[mine] = my_query
    width = weight_hbm.shape[0]
    weight[width:] = jnp.zeros((weight.shape[0] - width, weight.shape[1]), weight.dtype)

    load_table.wait()
    load_fresh.wait()

    def slot_at(kind, place, i):
        if kind == 0:
            return place * SIDE + 2 * i + place % 2
        return (2 * i + 1 - place % 2) * SIDE + place

    for kind in (0, 1):
        for place in range(SIDE):
            for i in range(HALF):
                send_kv[kind, place, i] = fresh[table_smem[0, slot_at(kind, place, i)]]
    for kind in (0, 1):
        recv_kv[kind, me[kind]] = send_kv[kind, me[kind]]

    pl.semaphore_wait(barrier, len(peers))

    q_copies = []
    for n, step in enumerate(FAR_FIRST):
        peer = at(z + step * parity, y + step * (1 - parity))
        q_copies.append(
            remote(query_all.at[mine], query_all.at[mine], q_send.at[n], q_recv.at[mine], peer)
        )
        q_copies[-1].start()
    kv_copies = []
    for n, step in enumerate(FAR_FIRST):
        for kind in (0, 1):
            there = lax.rem(me[kind] + step, SIDE)
            kv_copies.append(
                remote(
                    send_kv.at[kind, there],
                    recv_kv.at[kind, me[kind]],
                    kv_send.at[kind, n],
                    kv_recv.at[kind, me[kind]],
                    along(kind, step),
                )
            )
            kv_copies[-1].start()

    load_cache.wait()
    load_new.wait()
    load_len.wait()
    parts = []
    fill = fill_ref[0]
    for block in range(cache.shape[0] // CBLK):
        rows = pl.ds(block * CBLK, CBLK)
        position = block * CBLK + lax.broadcasted_iota(jnp.int32, (PAD, CBLK), 1)
        parts.append(
            attend(my_query, cache[rows, :D_HEAD], cache[rows, D_HEAD:], position < fill)
        )
    query_full = query_f32[...]
    new_rows = new_ref[0].astype(jnp.float32)
    step_of_row = lax.broadcasted_iota(jnp.int32, (PAD, 1), 0) // GROUP
    new_scores = [
        jnp.where(
            u <= step_of_row,
            jnp.sum(query_full * new_rows[u : u + 1, :D_HEAD], axis=1, keepdims=True) * SCALE,
            NONE,
        )
        for u in range(STEPS)
    ]
    new_top = functools.reduce(jnp.maximum, new_scores)
    new_weights = [
        jnp.where(u <= step_of_row, jnp.exp(new_scores[u] - new_top), 0.0) for u in range(STEPS)
    ]
    new_output = sum(
        new_weights[u].astype(jnp.bfloat16).astype(jnp.float32) * new_rows[u : u + 1, D_HEAD:]
        for u in range(STEPS)
    )
    parts.append((new_top, sum(new_weights), new_output))
    top, total, output = merge(parts)
    row_id = lax.broadcasted_iota(jnp.int32, (PAD, D_HEAD), 0)
    lane_id = lax.broadcasted_iota(jnp.int32, (PAD, D_HEAD), 1)
    index_of_mine = lax.rem(mine, HALF)
    own_lane = lane_id == row_id + index_of_mine * PAD
    cache_out[...] = output / total
    own_log = jnp.sum(
        jnp.where(own_lane, top + jnp.log(total), 0.0), axis=0, keepdims=True
    )
    own_lanes = lane_id[:1] // PAD == index_of_mine
    for kind in (0, 1):
        cache_log[kind : kind + 1] = jnp.where(
            jnp.logical_and(own_lanes, parity == kind), own_log, NONE
        )

    for n in range(2 * HALF - 1):
        if n < HALF - 1:
            came = parity * HALF + lax.rem(index_of_mine + 1 + n, HALF)
        else:
            came = (1 - parity) * HALF + n - (HALF - 1)
        remote(
            query_all.at[came], query_all.at[came], q_send.at[n], q_recv.at[came], any_peer
        ).wait_recv()
    for step in FAR_FIRST[::-1]:
        for kind in (0, 1):
            there = lax.rem(me[kind] + step, SIDE)
            remote(
                send_kv.at[kind, there],
                recv_kv.at[kind, there],
                kv_send.at[kind, 0],
                kv_recv.at[kind, there],
                any_peer,
            ).wait_recv()

    span = SIDE * 16
    position_id = lax.broadcasted_iota(jnp.int32, (span, D_HEAD), 0)
    positions = (
        (position_id // 16) * span + y * 16 + position_id % 16,
        z * span + position_id,
    )
    lane_slot = lax.broadcasted_iota(jnp.int32, (1, D_HEAD), 1) // PAD
    row8 = lax.broadcasted_iota(jnp.int32, (16, D_HEAD), 0)
    results = []
    own_shares = []
    for kind in (0, 1):
        lengths = jnp.zeros((1, D_HEAD), jnp.int32)
        for i in range(HALF):
            if kind == 0:
                slot = z * SIDE + 2 * i + z % 2
            else:
                slot = (2 * i + 1 - y % 2) * SIDE + y
            lengths = jnp.where(lane_slot == i, len_ref[table_smem[0, slot]], lengths)
        queries = query_all[kind * HALF : (kind + 1) * HALF].reshape(HALF * PAD, D_HEAD)
        every = lax.dot_general(
            recv_kv[kind, :, :, :, :D_HEAD].reshape(HALF * span, D_HEAD),
            queries,
            (((1,), (1,)), ((), ())),
            preferred_element_type=jnp.float32,
        ).reshape(SIDE, HALF, 16, D_HEAD)
        scores = every[:, 0]
        for i in range(1, HALF):
            scores = jnp.where(lane_slot[None] == i, every[:, i], scores)
        scores = scores.reshape(span, D_HEAD) * SCALE
        valid = positions[kind] < lengths
        own = cache_log[kind : kind + 1]
        top = jnp.maximum(
            jnp.max(jnp.where(valid, scores, NONE), axis=0, keepdims=True), own
        )
        weights = jnp.where(valid, jnp.exp(scores - top), 0.0)
        own_weight = jnp.exp(own - top)
        total = jnp.sum(weights, axis=0, keepdims=True) + own_weight
        share = 1.0 / total
        own_shares.append(own_weight * share)
        shares = (weights * share).T.astype(jnp.bfloat16)
        outputs = [
            jnp.dot(
                shares[i * PAD : (i + 1) * PAD],
                recv_kv[kind, :, i, :, D_HEAD:].reshape(span, D_HEAD),
                preferred_element_type=jnp.float32,
            )[:ROWS]
            for i in range(HALF)
        ]
        line = top + jnp.log(total)
        first = line.astype(jnp.bfloat16).astype(jnp.float32)
        second = (line - first).astype(jnp.bfloat16).astype(jnp.float32)
        third = line - first - second
        lines = jnp.where(
            row8 == 0,
            first,
            jnp.where(row8 == 1, second, jnp.where(row8 == 2, third, 0.0)),
        )
        results.append((outputs, lines))
    own_share = jnp.where(parity == 0, own_shares[0], own_shares[1])
    own_column = jnp.sum(jnp.where(own_lane, own_share, 0.0), axis=1, keepdims=True)
    own_part = (own_column * cache_out[...])[:ROWS]
    for kind in (0, 1):
        outputs, lines = results[kind]
        pieces[kind, me[1 - kind]] = jnp.concatenate(
            [
                jnp.where(mine == kind * HALF + i, own_part, 0.0) + outputs[i]
                for i in range(HALF)
            ]
            + [lines],
            axis=0,
        ).astype(jnp.bfloat16)

    o_copies = []
    for n, step in enumerate(FAR_FIRST):
        for kind in (0, 1):
            mine_here = me[1 - kind]
            o_copies.append(
                remote(
                    pieces.at[kind, mine_here],
                    pieces.at[kind, mine_here],
                    o_send.at[kind, n],
                    o_recv.at[kind, mine_here],
                    along(1 - kind, step),
                )
            )
            o_copies[-1].start()
    for step in FAR_FIRST[::-1]:
        for kind in (0, 1):
            there = lax.rem(me[1 - kind] + step, SIDE)
            remote(
                pieces.at[kind, there],
                pieces.at[kind, there],
                o_send.at[kind, 0],
                o_recv.at[kind, there],
                any_peer,
            ).wait_recv()

    for kind in (0, 1):
        arrived = [pieces[kind, src].astype(jnp.float32) for src in range(SIDE)]
        logs = jnp.concatenate(
            [jnp.sum(a[BAND:], axis=0, keepdims=True) for a in arrived], axis=0
        )
        weights = jnp.exp(logs - jnp.max(logs, axis=0, keepdims=True))
        weights = weights / jnp.sum(weights, axis=0, keepdims=True)
        columns = jnp.concatenate(
            [weights, jnp.zeros((D_HEAD - SIDE, D_HEAD), jnp.float32)], axis=0
        ).T
        rows = []
        for i in range(HALF):
            acc = None
            for src in range(SIDE):
                term = (
                    columns[i * PAD : i * PAD + ROWS, src : src + 1]
                    * arrived[src][i * ROWS : (i + 1) * ROWS]
                )
                acc = term if acc is None else acc + term
            rows.append(acc)
        gathered[kind, me[kind]] = jnp.concatenate(rows, axis=0).astype(jnp.bfloat16)

    g_copies = []
    for n, step in enumerate(FAR_FIRST):
        for kind in (0, 1):
            g_copies.append(
                remote(
                    gathered.at[kind, me[kind]],
                    gathered.at[kind, me[kind]],
                    g_send.at[kind, n],
                    g_recv.at[kind, me[kind]],
                    along(kind, step),
                )
            )
            g_copies[-1].start()
    load_weight.wait()
    for step in (0,) + FAR_FIRST[::-1]:
        for kind in (0, 1):
            there = lax.rem(me[kind] + step, SIDE)
            if step:
                remote(
                    gathered.at[kind, there],
                    gathered.at[kind, there],
                    g_send.at[kind, 0],
                    g_recv.at[kind, there],
                    any_peer,
                ).wait_recv()
            stage[pl.ds((kind * SIDE + there) * HALF, HALF)] = (
                gathered[kind, there].astype(jnp.float32).reshape(HALF, ROWS, D_HEAD)
            )

    for track in range(n_tracks):
        rows = stage[table_smem[1, track]]
        for t in range(STEPS):
            ordered[pl.ds((t * n_tracks + track) * GROUP, GROUP), :] = rows[
                t * GROUP : (t + 1) * GROUP
            ]
    product = None
    for g in range(GROUP):
        left = ordered[pl.ds(g, n_tracks * STEPS, stride=GROUP), :].astype(jnp.bfloat16)
        term = lax.dot_general(
            left,
            weight[:, g * D_HEAD : (g + 1) * D_HEAD],
            (((1,), (1,)), ((), ())),
            preferred_element_type=jnp.float32,
        )
        product = term if product is None else product + term
    parts = [product[t * n_tracks : (t + 1) * n_tracks] for t in range(STEPS)]
    lane = lax.broadcasted_iota(jnp.int32, (n_tracks, 128), 1)
    middle = pltpu.roll(parts[1], width, 1)
    last = pltpu.roll(parts[2], 2 * width - 128, 1)
    sums[head, :, :128] = jnp.where(lane < width, parts[0], middle).astype(jnp.bfloat16)
    sums[head, :, 128:] = jnp.where(lane < 2 * width - 128, middle, last).astype(jnp.bfloat16)

    s_copies = []
    for n, step in enumerate(HEAD_ORDER):
        s_copies.append(
            remote(sums.at[head], sums.at[head], s_send.at[n], s_recv.at[head], head_peer(step))
        )
        s_copies[-1].start()
    for step in HEAD_ORDER[::-1]:
        there = lax.rem(head + step, n_heads)
        remote(
            sums.at[there], sums.at[there], s_send.at[0], s_recv.at[there], any_peer
        ).wait_recv()
    summed = sums[0].astype(jnp.float32)
    for there in range(1, n_heads):
        summed = summed + sums[there].astype(jnp.float32)
    left, right = summed[:, :128], summed[:, 128:]
    split = 128 - width
    middle = jnp.where(lane < split, pltpu.roll(left, split, 1), pltpu.roll(right, split, 1))
    last = pltpu.roll(right, 256 - 2 * width, 1)
    for t, rows in enumerate((left, middle, last)):
        out_ref[t * n_tracks : (t + 1) * n_tracks] = rows[:, :width].astype(out_ref.dtype)

    for copy in q_copies + kv_copies + o_copies + g_copies + s_copies:
        copy.wait_send()


def shards(queries, new_kv, cache_kv, cache_fill, fresh_kv, fresh_len, owner_slot, out_weight):
    n_tracks, depth = fresh_kv.shape[0], fresh_kv.shape[1]
    width = out_weight.shape[1]
    vmem = pl.BlockSpec(memory_space=pltpu.VMEM)
    hbm = pl.BlockSpec(memory_space=pltpu.HBM)
    bf16, f32 = jnp.bfloat16, jnp.float32
    dma = pltpu.SemaphoreType.DMA
    out = pl.pallas_call(
        kernel,
        name="handoff_decode",
        out_shape=pltpu.VMEM((n_tracks * STEPS, width), bf16),
        in_specs=[pl.BlockSpec(memory_space=pltpu.SMEM)] + [hbm] * 7,
        out_specs=vmem,
        scratch_shapes=[
            pltpu.VMEM((1, n_tracks), jnp.int32),
            pltpu.SMEM((n_tracks,), jnp.int32),
            pltpu.VMEM(queries.shape, bf16),
            pltpu.VMEM(new_kv.shape, bf16),
            pltpu.VMEM(cache_kv.shape[1:], bf16),
            pltpu.VMEM(fresh_kv.shape, bf16),
            pltpu.VMEM((128, out_weight.shape[0]), bf16),
            pltpu.VMEM((8, 128), jnp.int32),
            pltpu.SMEM((8, 128), jnp.int32),
            pltpu.VMEM((PAD, D_HEAD), f32),
            pltpu.VMEM((2 * HALF, PAD, D_HEAD), bf16),
            pltpu.VMEM((2, SIDE, HALF, depth, 2 * D_HEAD), bf16),
            pltpu.VMEM((2, SIDE, HALF, depth, 2 * D_HEAD), bf16),
            pltpu.VMEM((PAD, D_HEAD), f32),
            pltpu.VMEM((8, D_HEAD), f32),
            pltpu.VMEM((2, SIDE, PIECE, D_HEAD), bf16),
            pltpu.VMEM((2, SIDE, HALF * ROWS, D_HEAD), bf16),
            pltpu.VMEM((n_tracks, ROWS, D_HEAD), f32),
            pltpu.VMEM((n_tracks * ROWS, D_HEAD), f32),
            pltpu.VMEM((8, n_tracks, 256), bf16),
            dma((8,)),
            dma((SIDE - 1,)),
            dma((2 * HALF,)),
            dma((2, SIDE - 1)),
            dma((2, SIDE)),
            dma((2, SIDE - 1)),
            dma((2, SIDE)),
            dma((2, SIDE - 1)),
            dma((2, SIDE)),
            dma((7,)),
            dma((8,)),
        ],
        compiler_params=pltpu.CompilerParams(
            collective_id=0, has_side_effects=True, vmem_limit_bytes=32 * 1024 * 1024
        ),
    )(
        cache_fill,
        *(
            pltpu.with_memory_space_constraint(operand, pltpu.HBM)
            for operand in (
                owner_slot[None, :],
                fresh_len,
                queries,
                new_kv,
                cache_kv[0],
                fresh_kv,
                out_weight.T,
            )
        )
    )
    return out.reshape(STEPS, n_tracks, width).transpose(1, 0, 2)


def solution(mesh):
    in_specs = (
        P("stream", None, "head"),
        P("stream", None, "head"),
        P("stream", None, "head"),
        P("stream"),
        P(None, "stream", "head"),
        P(),
        P(),
        P("head", "stream"),
    )
    out_specs = P(None, None, "stream")
    return jax.shard_map(shards, mesh=mesh, in_specs=in_specs, out_specs=out_specs, check_vma=False)
```

time: 55 us -> 47.5 us (0.86)
  local copies, waits for them, and re-layouts: 5.16 us -> 0.62 us
  Pallas kernels: 48.9 us -> 46.1 us
    unnamed x15 -> x1, local copies, waits for them, and re-layouts: 5.16 us -> 0.62 us
    pallas_call x1, Pallas kernels: 48.9 us -> 46.1 us  [shards(): pl.pallas_call(kernel, name='handoff_decode', out_shape=pltpu.VMEM((n_tra...]
where the time goes in v2:
time: 47.5 us; the launch traced here: 47.4 us
  Pallas kernels  46.1 us (97%)
  between operations  0.66 us (1%)
  local copies, waits for them, and re-layouts  0.62 us (1%)
    pallas_call x1, Pallas kernels, shards(): pl.pallas_call(kernel, name='handoff_decode', out_shape=pltpu.VMEM((n_tra...  46.1 us

profile of v2, /device:TPU:1, one launch (start us, length us, event | category | flops | bytes accessed | tf_op | source)
XLA Modules:
  0.0 47.4 jit_solution(14756330986754957261)
XLA Ops:
  0.7 46.1 %handoff_decode.1 = bf16[192,80]{1,0:T(8,128)(2,1)S(1)} custom-call(s32[1]{0:T(128)S(6)} %copy.11.fill_ref, s32[1,64]{1,0:T(1,128)} %bitcast.9, s32[64]{0:T(128)} %len_hbm.1, bf16[1,3,1024]{2,1,0:T(4,128)(2,1)} %query_hbm.1, bf16[1,3,256]{2,1,0:T(4,128)(2,1)} %new_hbm.1, bf16[2048,256]{1,0:T(8,128)(2,1)} %bitcast.7, bf16[64,16,256]{2,1,0:T(8,128)(2,1)} %fresh_hbm.1, ...), custom_call_target="tpu_custom_call" | custom-call | tf_op jit(solution)/shard_map/handoff_decode/pallas_call | solution.py:484
  46.8 0.6 %copy.10 = bf16[64,3,80]{2,0,1:T(8,128)(2,1)} copy(bf16[64,3,80]{2,0,1:T(8,128)(2,1)S(1)} %bitcast.6) | data formatting | bytes 61440

commit v3 on v2

--- a/solution.py
+++ b/solution.py
@@ -15,7 +15,9 @@
 CBLK = 512
 SIDE = 8
 HALF = 4
-BAND = HALF * ROWS
+PAIR = 2
+CHUNKS = HALF // PAIR
+BAND = PAIR * ROWS
 PIECE = BAND + 16
 NONE = -1e30
 SCALE = D_HEAD**-0.5
@@ -151,8 +153,8 @@
     owner_z, owner_y = owner // SIDE, owner % SIDE
     place_row = jnp.where(
         (owner_z + owner_y) % 2 == 0,
-        owner_z * HALF + owner_y // 2,
-        SIDE * HALF + owner_y * HALF + owner_z // 2,
+        owner_y // 4 * 32 + owner_z * PAIR + owner_y // 2 % PAIR,
+        owner_z // 4 * 32 + 16 + owner_y * PAIR + owner_z // 2 % PAIR,
     )
     table[...] = jnp.zeros_like(table)
     table[0:1, 0:n_tracks] = track_row
@@ -168,7 +170,9 @@
             :, g * D_HEAD : (g + 1) * D_HEAD
         ]
     parity = (z + y) % 2
-    mine = jnp.where(parity == 0, y // 2, HALF + z // 2)
+    my_index = jnp.where(parity == 0, y // 2, z // 2)
+    my_chunk, my_group = my_index // PAIR, parity * PAIR + my_index % PAIR
+    mine = my_chunk * 2 * PAIR + my_group
     my_query = query_f32[...].astype(jnp.bfloat16)
     query_all[mine] = my_query
     width = weight_hbm.shape[0]
@@ -182,12 +186,15 @@
             return place * SIDE + 2 * i + place % 2
         return (2 * i + 1 - place % 2) * SIDE + place
 
-    for kind in (0, 1):
-        for place in range(SIDE):
-            for i in range(HALF):
-                send_kv[kind, place, i] = fresh[table_smem[0, slot_at(kind, place, i)]]
-    for kind in (0, 1):
-        recv_kv[kind, me[kind]] = send_kv[kind, me[kind]]
+    for chunk in range(CHUNKS):
+        for kind in (0, 1):
+            for place in range(SIDE):
+                for j in range(PAIR):
+                    slot = slot_at(kind, place, chunk * PAIR + j)
+                    send_kv[chunk, kind, place, j] = fresh[table_smem[0, slot]]
+    for chunk in range(CHUNKS):
+        for kind in (0, 1):
+            recv_kv[chunk, kind, me[kind]] = send_kv[chunk, kind, me[kind]]
 
     pl.semaphore_wait(barrier, len(peers))
 
@@ -198,20 +205,44 @@
             remote(query_all.at[mine], query_all.at[mine], q_send.at[n], q_recv.at[mine], peer)
         )
         q_copies[-1].start()
+    def spread(buffer, source, chunk, send_sems, recv_sems, turn):
+        copies = []
+        for n, step in enumerate(FAR_FIRST):
+            for kind in (0, 1):
+                axis = kind ^ turn
+                here = me[axis]
+                from_ref = (
+                    buffer.at[chunk, kind, here]
+                    if source is None
+                    else source.at[chunk, kind, lax.rem(here + step, SIDE)]
+                )
+                copies.append(
+                    remote(
+                        from_ref,
+                        buffer.at[chunk, kind, here],
+                        send_sems.at[chunk, kind, n],
+                        recv_sems.at[chunk, kind, here],
+                        along(axis, step),
+                    )
+                )
+                copies[-1].start()
+        return copies
+
+    def arrival(buffer, chunk, kind, there, send_sems, recv_sems):
+        block = buffer.at[chunk, kind, there]
+        remote(
+            block, block, send_sems.at[chunk, kind, 0], recv_sems.at[chunk, kind, there], any_peer
+        ).wait_recv()
+
+    def collect(buffer, chunk, send_sems, recv_sems, turn):
+        for step in FAR_FIRST[::-1]:
+            for kind in (0, 1):
+                there = lax.rem(me[kind ^ turn] + step, SIDE)
+                arrival(buffer, chunk, kind, there, send_sems, recv_sems)
+
     kv_copies = []
-    for n, step in enumerate(FAR_FIRST):
-        for kind in (0, 1):
-            there = lax.rem(me[kind] + step, SIDE)
-            kv_copies.append(
-                remote(
-                    send_kv.at[kind, there],
-                    recv_kv.at[kind, me[kind]],
-                    kv_send.at[kind, n],
-                    kv_recv.at[kind, me[kind]],
-                    along(kind, step),
-                )
-            )
-            kv_copies[-1].start()
+    for chunk in range(CHUNKS):
+        kv_copies += spread(recv_kv, send_kv, chunk, kv_send, kv_recv, 0)
 
     load_cache.wait()
     load_new.wait()
@@ -247,68 +278,56 @@
     top, total, output = merge(parts)
     row_id = lax.broadcasted_iota(jnp.int32, (PAD, D_HEAD), 0)
     lane_id = lax.broadcasted_iota(jnp.int32, (PAD, D_HEAD), 1)
-    index_of_mine = lax.rem(mine, HALF)
-    own_lane = lane_id == row_id + index_of_mine * PAD
+    own_lane = lane_id == row_id + my_group * PAD
     cache_out[...] = output / total
     own_log = jnp.sum(
         jnp.where(own_lane, top + jnp.log(total), 0.0), axis=0, keepdims=True
     )
-    own_lanes = lane_id[:1] // PAD == index_of_mine
-    for kind in (0, 1):
-        cache_log[kind : kind + 1] = jnp.where(
-            jnp.logical_and(own_lanes, parity == kind), own_log, NONE
+    own_lanes = lane_id[:1] // PAD == my_group
+    for chunk in range(CHUNKS):
+        cache_log[chunk : chunk + 1] = jnp.where(
+            jnp.logical_and(own_lanes, my_chunk == chunk), own_log, NONE
         )
 
     for n in range(2 * HALF - 1):
-        if n < HALF - 1:
-            came = parity * HALF + lax.rem(index_of_mine + 1 + n, HALF)
-        else:
-            came = (1 - parity) * HALF + n - (HALF - 1)
+        came = lax.rem(mine + 1 + n, 2 * HALF)
         remote(
             query_all.at[came], query_all.at[came], q_send.at[n], q_recv.at[came], any_peer
         ).wait_recv()
-    for step in FAR_FIRST[::-1]:
-        for kind in (0, 1):
-            there = lax.rem(me[kind] + step, SIDE)
-            remote(
-                send_kv.at[kind, there],
-                recv_kv.at[kind, there],
-                kv_send.at[kind, 0],
-                kv_recv.at[kind, there],
-                any_peer,
-            ).wait_recv()
 
     span = SIDE * 16
     position_id = lax.broadcasted_iota(jnp.int32, (span, D_HEAD), 0)
-    positions = (
+    lane_group = lax.broadcasted_iota(jnp.int32, (1, D_HEAD), 1) // PAD
+    positions = jnp.where(
+        lane_group < PAIR,
         (position_id // 16) * span + y * 16 + position_id % 16,
         z * span + position_id,
     )
-    lane_slot = lax.broadcasted_iota(jnp.int32, (1, D_HEAD), 1) // PAD
-    row8 = lax.broadcasted_iota(jnp.int32, (16, D_HEAD), 0)
-    results = []
-    own_shares = []
-    for kind in (0, 1):
+    row16 = lax.broadcasted_iota(jnp.int32, (16, D_HEAD), 0)
+    groups = [(kind, j) for kind in (0, 1) for j in range(PAIR)]
+    o_copies = []
+    for chunk in range(CHUNKS):
         lengths = jnp.zeros((1, D_HEAD), jnp.int32)
-        for i in range(HALF):
+        for n, (kind, j) in enumerate(groups):
+            i = chunk * PAIR + j
             if kind == 0:
                 slot = z * SIDE + 2 * i + z % 2
             else:
                 slot = (2 * i + 1 - y % 2) * SIDE + y
-            lengths = jnp.where(lane_slot == i, len_ref[table_smem[0, slot]], lengths)
-        queries = query_all[kind * HALF : (kind + 1) * HALF].reshape(HALF * PAD, D_HEAD)
+            lengths = jnp.where(lane_group == n, len_ref[table_smem[0, slot]], lengths)
+        valid = positions < lengths
+        collect(recv_kv, chunk, kv_send, kv_recv, 0)
         every = lax.dot_general(
-            recv_kv[kind, :, :, :, :D_HEAD].reshape(HALF * span, D_HEAD),
-            queries,
+            recv_kv[chunk, :, :, :, :, :D_HEAD].reshape(2 * PAIR * span, D_HEAD),
+            query_all[chunk * 2 * PAIR : (chunk + 1) * 2 * PAIR].reshape(D_HEAD, D_HEAD),
             (((1,), (1,)), ((), ())),
             preferred_element_type=jnp.float32,
-        ).reshape(SIDE, HALF, 16, D_HEAD)
-        scores = every[:, 0]
-        for i in range(1, HALF):
-            scores = jnp.where(lane_slot[None] == i, every[:, i], scores)
+        ).reshape(2, SIDE, PAIR, 16, D_HEAD)
+        scores = every[0, :, 0]
+        for n, (kind, j) in enumerate(groups[1:]):
+            scores = jnp.where(lane_group[None] == n + 1, every[kind, :, j], scores)
         scores = scores.reshape(span, D_HEAD) * SCALE
-        valid = positions[kind] < lengths
-        own = cache_log[kind : kind + 1]
+        own = cache_log[chunk : chunk + 1]
         top = jnp.maximum(
             jnp.max(jnp.where(valid, scores, NONE), axis=0, keepdims=True), own
         )
@@ -316,115 +335,82 @@
         own_weight = jnp.exp(own - top)
         total = jnp.sum(weights, axis=0, keepdims=True) + own_weight
         share = 1.0 / total
-        own_shares.append(own_weight * share)
         shares = (weights * share).T.astype(jnp.bfloat16)
         outputs = [
             jnp.dot(
-                shares[i * PAD : (i + 1) * PAD],
-                recv_kv[kind, :, i, :, D_HEAD:].reshape(span, D_HEAD),
+                shares[n * PAD : (n + 1) * PAD],
+                recv_kv[chunk, kind, :, j, :, D_HEAD:].reshape(span, D_HEAD),
                 preferred_element_type=jnp.float32,
             )[:ROWS]
-            for i in range(HALF)
+            for n, (kind, j) in enumerate(groups)
+        ]
+        own_column = jnp.sum(
+            jnp.where(own_lane, own_weight * share, 0.0), axis=1, keepdims=True
+        )
+        own_part = (own_column * cache_out[...])[:ROWS]
+        outputs = [
+            output + jnp.where(mine == chunk * 2 * PAIR + n, own_part, 0.0)
+            for n, output in enumerate(outputs)
         ]
         line = top + jnp.log(total)
         first = line.astype(jnp.bfloat16).astype(jnp.float32)
         second = (line - first).astype(jnp.bfloat16).astype(jnp.float32)
         third = line - first - second
         lines = jnp.where(
-            row8 == 0,
+            row16 == 0,
             first,
-            jnp.where(row8 == 1, second, jnp.where(row8 == 2, third, 0.0)),
-        )
-        results.append((outputs, lines))
-    own_share = jnp.where(parity == 0, own_shares[0], own_shares[1])
-    own_column = jnp.sum(jnp.where(own_lane, own_share, 0.0), axis=1, keepdims=True)
-    own_part = (own_column * cache_out[...])[:ROWS]
-    for kind in (0, 1):
-        outputs, lines = results[kind]
-        pieces[kind, me[1 - kind]] = jnp.concatenate(
-            [
-                jnp.where(mine == kind * HALF + i, own_part, 0.0) + outputs[i]
-                for i in range(HALF)
-            ]
-            + [lines],
-            axis=0,
-        ).astype(jnp.bfloat16)
-
-    o_copies = []
-    for n, step in enumerate(FAR_FIRST):
+            jnp.where(row16 == 1, second, jnp.where(row16 == 2, third, 0.0)),
+        )
         for kind in (0, 1):
-            mine_here = me[1 - kind]
-            o_copies.append(
-                remote(
-                    pieces.at[kind, mine_here],
-                    pieces.at[kind, mine_here],
-                    o_send.at[kind, n],
-                    o_recv.at[kind, mine_here],
-                    along(1 - kind, step),
-                )
-            )
-            o_copies[-1].start()
-    for step in FAR_FIRST[::-1]:
-        for kind in (0, 1):
-            there = lax.rem(me[1 - kind] + step, SIDE)
-            remote(
-                pieces.at[kind, there],
-                pieces.at[kind, there],
-                o_send.at[kind, 0],
-                o_recv.at[kind, there],
-                any_peer,
-            ).wait_recv()
-
-    for kind in (0, 1):
-        arrived = [pieces[kind, src].astype(jnp.float32) for src in range(SIDE)]
-        logs = jnp.concatenate(
-            [jnp.sum(a[BAND:], axis=0, keepdims=True) for a in arrived], axis=0
-        )
+            pieces[chunk, kind, me[1 - kind]] = jnp.concatenate(
+                outputs[kind * PAIR : (kind + 1) * PAIR] + [lines], axis=0
+            ).astype(jnp.bfloat16)
+        o_copies += spread(pieces, None, chunk, o_send, o_recv, 1)
+
+    g_copies = []
+    for chunk in range(CHUNKS):
+        collect(pieces, chunk, o_send, o_recv, 1)
+        arrived = [
+            [pieces[chunk, kind, src].astype(jnp.float32) for src in range(SIDE)]
+            for kind in (0, 1)
+        ]
+        logs = [
+            jnp.concatenate([jnp.sum(a[BAND:], axis=0, keepdims=True) for a in some], axis=0)
+            for some in arrived
+        ]
+        logs = jnp.where(lane_group < PAIR, logs[0], logs[1])
         weights = jnp.exp(logs - jnp.max(logs, axis=0, keepdims=True))
         weights = weights / jnp.sum(weights, axis=0, keepdims=True)
         columns = jnp.concatenate(
             [weights, jnp.zeros((D_HEAD - SIDE, D_HEAD), jnp.float32)], axis=0
         ).T
         rows = []
-        for i in range(HALF):
+        for n, (kind, j) in enumerate(groups):
             acc = None
             for src in range(SIDE):
                 term = (
-                    columns[i * PAD : i * PAD + ROWS, src : src + 1]
-                    * arrived[src][i * ROWS : (i + 1) * ROWS]
+                    columns[n * PAD : n * PAD + ROWS, src : src + 1]
+                    * arrived[kind][src][j * ROWS : (j + 1) * ROWS]
                 )
                 acc = term if acc is None else acc + term
             rows.append(acc)
-        gathered[kind, me[kind]] = jnp.concatenate(rows, axis=0).astype(jnp.bfloat16)
-
-    g_copies = []
-    for n, step in enumerate(FAR_FIRST):
         for kind in (0, 1):
-            g_copies.append(
-                remote(
-                    gathered.at[kind, me[kind]],
-                    gathered.at[kind, me[kind]],
-                    g_send.at[kind, n],
-                    g_recv.at[kind, me[kind]],
-                    along(kind, step),
+            gathered[chunk, kind, me[kind]] = jnp.concatenate(
+                rows[kind * PAIR : (kind + 1) * PAIR], axis=0
+            ).astype(jnp.bfloat16)
+        g_copies += spread(gathered, None, chunk, g_send, g_recv, 0)
+
+    load_weight.wait()
+    for chunk in range(CHUNKS):
+        for step in (0,) + FAR_FIRST[::-1]:
+            for kind in (0, 1):
+                there = lax.rem(me[kind] + step, SIDE)
+                if step:
+                    arrival(gathered, chunk, kind, there, g_send, g_recv)
+                place = ((chunk * 2 + kind) * SIDE + there) * PAIR
+                stage[pl.ds(place, PAIR)] = (
+                    gathered[chunk, kind, there].astype(jnp.float32).reshape(PAIR, ROWS, D_HEAD)
                 )
-            )
-            g_copies[-1].start()
-    load_weight.wait()
-    for step in (0,) + FAR_FIRST[::-1]:
-        for kind in (0, 1):
-            there = lax.rem(me[kind] + step, SIDE)
-            if step:
-                remote(
-                    gathered.at[kind, there],
-                    gathered.at[kind, there],
-                    g_send.at[kind, 0],
-                    g_recv.at[kind, there],
-                    any_peer,
-                ).wait_recv()
-            stage[pl.ds((kind * SIDE + there) * HALF, HALF)] = (
-                gathered[kind, there].astype(jnp.float32).reshape(HALF, ROWS, D_HEAD)
-            )
 
     for track in range(n_tracks):
         rows = stage[table_smem[1, track]]
@@ -499,24 +485,24 @@
             pltpu.SMEM((8, 128), jnp.int32),
             pltpu.VMEM((PAD, D_HEAD), f32),
             pltpu.VMEM((2 * HALF, PAD, D_HEAD), bf16),
-            pltpu.VMEM((2, SIDE, HALF, depth, 2 * D_HEAD), bf16),
-            pltpu.VMEM((2, SIDE, HALF, depth, 2 * D_HEAD), bf16),
+            pltpu.VMEM((CHUNKS, 2, SIDE, PAIR, depth, 2 * D_HEAD), bf16),
+            pltpu.VMEM((CHUNKS, 2, SIDE, PAIR, depth, 2 * D_HEAD), bf16),
             pltpu.VMEM((PAD, D_HEAD), f32),
             pltpu.VMEM((8, D_HEAD), f32),
-            pltpu.VMEM((2, SIDE, PIECE, D_HEAD), bf16),
-            pltpu.VMEM((2, SIDE, HALF * ROWS, D_HEAD), bf16),
+            pltpu.VMEM((CHUNKS, 2, SIDE, PIECE, D_HEAD), bf16),
+            pltpu.VMEM((CHUNKS, 2, SIDE, BAND, D_HEAD), bf16),
             pltpu.VMEM((n_tracks, ROWS, D_HEAD), f32),
             pltpu.VMEM((n_tracks * ROWS, D_HEAD), f32),
             pltpu.VMEM((8, n_tracks, 256), bf16),
             dma((8,)),
             dma((SIDE - 1,)),
             dma((2 * HALF,)),
-            dma((2, SIDE - 1)),
-            dma((2, SIDE)),
-            dma((2, SIDE - 1)),
-            dma((2, SIDE)),
-            dma((2, SIDE - 1)),
-            dma((2, SIDE)),
+            dma((CHUNKS, 2, SIDE - 1)),
+            dma((CHUNKS, 2, SIDE)),
+            dma((CHUNKS, 2, SIDE - 1)),
+            dma((CHUNKS, 2, SIDE)),
+            dma((CHUNKS, 2, SIDE - 1)),
+            dma((CHUNKS, 2, SIDE)),
             dma((7,)),
             dma((8,)),
         ],

time: 47.5 us -> 46.1 us (0.971)
  Pallas kernels: 46.1 us -> 44.7 us
    pallas_call x1, Pallas kernels: 46.1 us -> 44.7 us  [shards(): pl.pallas_call(kernel, name='handoff_decode', out_shape=pltpu.VMEM((n_tra...]
where the time goes in v3:
time: 46.1 us; the launch traced here: 45.9 us
  Pallas kernels  44.7 us (97%)
  between operations  0.66 us (1%)
  local copies, waits for them, and re-layouts  0.62 us (1%)
    pallas_call x1, Pallas kernels, shards(): pl.pallas_call(kernel, name='handoff_decode', out_shape=pltpu.VMEM((n_tra...  44.7 us

profile of v3, /device:TPU:1, one launch (start us, length us, event | category | flops | bytes accessed | tf_op | source)
XLA Modules:
  0.0 45.9 jit_solution(12453073960067256044)
XLA Ops:
  0.7 44.7 %handoff_decode.1 = bf16[192,80]{1,0:T(8,128)(2,1)S(1)} custom-call(s32[1]{0:T(128)S(6)} %copy.11.fill_ref, s32[1,64]{1,0:T(1,128)} %bitcast.9, s32[64]{0:T(128)} %len_hbm.1, bf16[1,3,1024]{2,1,0:T(4,128)(2,1)} %query_hbm.1, bf16[1,3,256]{2,1,0:T(4,128)(2,1)} %new_hbm.1, bf16[2048,256]{1,0:T(8,128)(2,1)} %bitcast.7, bf16[64,16,256]{2,1,0:T(8,128)(2,1)} %fresh_hbm.1, ...), custom_call_target="tpu_custom_call" | custom-call | tf_op jit(solution)/shard_map/handoff_decode/pallas_call | solution.py:470
  45.3 0.6 %copy.10 = bf16[64,3,80]{2,0,1:T(8,128)(2,1)} copy(bf16[64,3,80]{2,0,1:T(8,128)(2,1)S(1)} %bitcast.6) | data formatting | bytes 61440

commit v4 on v3

--- a/solution.py
+++ b/solution.py
@@ -87,8 +87,8 @@
     pieces,
     gathered,
     stage,
-    ordered,
     sums,
+    pick,
     local_sem,
     q_send,
     q_recv,
@@ -156,11 +156,11 @@
         owner_y // 4 * 32 + owner_z * PAIR + owner_y // 2 % PAIR,
         owner_z // 4 * 32 + 16 + owner_y * PAIR + owner_z // 2 % PAIR,
     )
-    table[...] = jnp.zeros_like(table)
-    table[0:1, 0:n_tracks] = track_row
-    table[1:2, 0:n_tracks] = place_row
+    table[...] = track_row
     load_table = pltpu.make_async_copy(table, table_smem, local_sem.at[7])
     load_table.start()
+    picked = slot_of == place_row
+    pick[...] = picked.astype(jnp.float32).T.astype(jnp.bfloat16)
 
     query_f32[...] = jnp.zeros_like(query_f32)
     load_query.wait()
@@ -401,55 +401,76 @@
         g_copies += spread(gathered, None, chunk, g_send, g_recv, 0)
 
     load_weight.wait()
+    s_copies = []
+    per_chunk = n_tracks // CHUNKS
+    lane = lax.broadcasted_iota(jnp.int32, (per_chunk, 128), 1)
     for chunk in range(CHUNKS):
         for step in (0,) + FAR_FIRST[::-1]:
             for kind in (0, 1):
                 there = lax.rem(me[kind] + step, SIDE)
                 if step:
                     arrival(gathered, chunk, kind, there, g_send, g_recv)
-                place = ((chunk * 2 + kind) * SIDE + there) * PAIR
-                stage[pl.ds(place, PAIR)] = (
-                    gathered[chunk, kind, there].astype(jnp.float32).reshape(PAIR, ROWS, D_HEAD)
+                place = ((chunk * 2 + kind) * SIDE + there) * BAND
+                stage[pl.ds(place, BAND), :] = gathered[chunk, kind, there].astype(jnp.float32)
+        product = None
+        for g in range(GROUP):
+            left = jnp.concatenate(
+                [
+                    stage[
+                        pl.ds(chunk * per_chunk * ROWS + t * GROUP + g, per_chunk, stride=ROWS), :
+                    ]
+                    for t in range(STEPS)
+                ],
+                axis=0,
+            ).astype(jnp.bfloat16)
+            term = lax.dot_general(
+                left,
+                weight[:, g * D_HEAD : (g + 1) * D_HEAD],
+                (((1,), (1,)), ((), ())),
+                preferred_element_type=jnp.float32,
+            )
+            product = term if product is None else product + term
+        parts = [product[t * per_chunk : (t + 1) * per_chunk] for t in range(STEPS)]
+        middle = pltpu.roll(parts[1], width, 1)
+        last = pltpu.roll(parts[2], 2 * width - 128, 1)
+        sums[chunk, head, :, :128] = jnp.where(lane < width, parts[0], middle).astype(jnp.bfloat16)
+        sums[chunk, head, :, 128:] = jnp.where(lane < 2 * width - 128, middle, last).astype(
+            jnp.bfloat16
+        )
+        for n, step in enumerate(HEAD_ORDER):
+            s_copies.append(
+                remote(
+                    sums.at[chunk, head],
+                    sums.at[chunk, head],
+                    s_send.at[chunk, n],
+                    s_recv.at[chunk, head],
+                    head_peer(step),
                 )
-
-    for track in range(n_tracks):
-        rows = stage[table_smem[1, track]]
-        for t in range(STEPS):
-            ordered[pl.ds((t * n_tracks + track) * GROUP, GROUP), :] = rows[
-                t * GROUP : (t + 1) * GROUP
-            ]
-    product = None
-    for g in range(GROUP):
-        left = ordered[pl.ds(g, n_tracks * STEPS, stride=GROUP), :].astype(jnp.bfloat16)
-        term = lax.dot_general(
-            left,
-            weight[:, g * D_HEAD : (g + 1) * D_HEAD],
-            (((1,), (1,)), ((), ())),
+            )
+            s_copies[-1].start()
+
+    decoded = None
+    for chunk in range(CHUNKS):
+        for step in HEAD_ORDER[::-1]:
+            there = lax.rem(head + step, n_heads)
+            remote(
+                sums.at[chunk, there],
+                sums.at[chunk, there],
+                s_send.at[chunk, 0],
+                s_recv.at[chunk, there],
+                any_peer,
+            ).wait_recv()
+        summed = sums[chunk, 0].astype(jnp.float32)
+        for there in range(1, n_heads):
+            summed = summed + sums[chunk, there].astype(jnp.float32)
+        term = jnp.dot(
+            pick[:, chunk * per_chunk : (chunk + 1) * per_chunk],
+            summed.astype(jnp.bfloat16),
             preferred_element_type=jnp.float32,
         )
-        product = term if product is None else product + term
-    parts = [product[t * n_tracks : (t + 1) * n_tracks] for t in range(STEPS)]
+        decoded = term if decoded is None else decoded + term
     lane = lax.broadcasted_iota(jnp.int32, (n_tracks, 128), 1)
-    middle = pltpu.roll(parts[1], width, 1)
-    last = pltpu.roll(parts[2], 2 * width - 128, 1)
-    sums[head, :, :128] = jnp.where(lane < width, parts[0], middle).astype(jnp.bfloat16)
-    sums[head, :, 128:] = jnp.where(lane < 2 * width - 128, middle, last).astype(jnp.bfloat16)
-
-    s_copies = []
-    for n, step in enumerate(HEAD_ORDER):
-        s_copies.append(
-            remote(sums.at[head], sums.at[head], s_send.at[n], s_recv.at[head], head_peer(step))
-        )
-        s_copies[-1].start()
-    for step in HEAD_ORDER[::-1]:
-        there = lax.rem(head + step, n_heads)
-        remote(
-            sums.at[there], sums.at[there], s_send.at[0], s_recv.at[there], any_peer
-        ).wait_recv()
-    summed = sums[0].astype(jnp.float32)
-    for there in range(1, n_heads):
-        summed = summed + sums[there].astype(jnp.float32)
-    left, right = summed[:, :128], summed[:, 128:]
+    left, right = decoded[:, :128], decoded[:, 128:]
     split = 128 - width
     middle = jnp.where(lane < split, pltpu.roll(left, split, 1), pltpu.roll(right, split, 1))
     last = pltpu.roll(right, 256 - 2 * width, 1)
@@ -481,8 +502,8 @@
             pltpu.VMEM(cache_kv.shape[1:], bf16),
             pltpu.VMEM(fresh_kv.shape, bf16),
             pltpu.VMEM((128, out_weight.shape[0]), bf16),
-            pltpu.VMEM((8, 128), jnp.int32),
-            pltpu.SMEM((8, 128), jnp.int32),
+            pltpu.VMEM((1, n_tracks), jnp.int32),
+            pltpu.SMEM((1, n_tracks), jnp.int32),
             pltpu.VMEM((PAD, D_HEAD), f32),
             pltpu.VMEM((2 * HALF, PAD, D_HEAD), bf16),
             pltpu.VMEM((CHUNKS, 2, SIDE, PAIR, depth, 2 * D_HEAD), bf16),
@@ -491,9 +512,9 @@
             pltpu.VMEM((8, D_HEAD), f32),
             pltpu.VMEM((CHUNKS, 2, SIDE, PIECE, D_HEAD), bf16),
             pltpu.VMEM((CHUNKS, 2, SIDE, BAND, D_HEAD), bf16),
-            pltpu.VMEM((n_tracks, ROWS, D_HEAD), f32),
             pltpu.VMEM((n_tracks * ROWS, D_HEAD), f32),
-            pltpu.VMEM((8, n_tracks, 256), bf16),
+            pltpu.VMEM((CHUNKS, 8, n_tracks // CHUNKS, 256), bf16),
+            pltpu.VMEM((n_tracks, n_tracks), bf16),
             dma((8,)),
             dma((SIDE - 1,)),
             dma((2 * HALF,)),
@@ -503,8 +524,8 @@
             dma((CHUNKS, 2, SIDE)),
             dma((CHUNKS, 2, SIDE - 1)),
             dma((CHUNKS, 2, SIDE)),
-            dma((7,)),
-            dma((8,)),
+            dma((CHUNKS, 7)),
+            dma((CHUNKS, 8)),
         ],
         compiler_params=pltpu.CompilerParams(
             collective_id=0, has_side_effects=True, vmem_limit_bytes=32 * 1024 * 1024

time: 46.1 us -> 45.7 us (level)
  no operation moved by 1% of the time
where the time goes in v4:
time: 45.7 us; the launch traced here: 45.6 us
  Pallas kernels  44.3 us (97%)
  between operations  0.66 us (1%)
  local copies, waits for them, and re-layouts  0.62 us (1%)
    pallas_call x1, Pallas kernels, shards(): pl.pallas_call(kernel, name='handoff_decode', out_shape=pltpu.VMEM((n_tra...  44.3 us

profile of v4, /device:TPU:1, one launch (start us, length us, event | category | flops | bytes accessed | tf_op | source)
XLA Modules:
  0.0 45.6 jit_solution(8137206761998693887)
XLA Ops:
  0.7 44.3 %handoff_decode.1 = bf16[192,80]{1,0:T(8,128)(2,1)S(1)} custom-call(s32[1]{0:T(128)S(6)} %copy.11.fill_ref, s32[1,64]{1,0:T(1,128)} %bitcast.9, s32[64]{0:T(128)} %len_hbm.1, bf16[1,3,1024]{2,1,0:T(4,128)(2,1)} %query_hbm.1, bf16[1,3,256]{2,1,0:T(4,128)(2,1)} %new_hbm.1, bf16[2048,256]{1,0:T(8,128)(2,1)} %bitcast.7, bf16[64,16,256]{2,1,0:T(8,128)(2,1)} %fresh_hbm.1, ...), custom_call_target="tpu_custom_call" | custom-call | tf_op jit(solution)/shard_map/handoff_decode/pallas_call | solution.py:491
  44.9 0.6 %copy.10 = bf16[64,3,80]{2,0,1:T(8,128)(2,1)} copy(bf16[64,3,80]{2,0,1:T(8,128)(2,1)S(1)} %bitcast.6) | data formatting | bytes 61440

commit v5 on v4

--- a/solution.py
+++ b/solution.py
@@ -191,58 +191,41 @@
             for place in range(SIDE):
                 for j in range(PAIR):
                     slot = slot_at(kind, place, chunk * PAIR + j)
-                    send_kv[chunk, kind, place, j] = fresh[table_smem[0, slot]]
+                    send_kv[chunk, kind * SIDE + place, j] = fresh[table_smem[0, slot]]
     for chunk in range(CHUNKS):
         for kind in (0, 1):
-            recv_kv[chunk, kind, me[kind]] = send_kv[chunk, kind, me[kind]]
+            here = kind * SIDE + me[kind]
+            recv_kv[chunk, here] = send_kv[chunk, here]
 
     pl.semaphore_wait(barrier, len(peers))
 
-    q_copies = []
-    for n, step in enumerate(FAR_FIRST):
+    def settle(view, send_sem, recv_sem):
+        return remote(view, view, send_sem, recv_sem, any_peer)
+
+    for step in FAR_FIRST:
         peer = at(z + step * parity, y + step * (1 - parity))
-        q_copies.append(
-            remote(query_all.at[mine], query_all.at[mine], q_send.at[n], q_recv.at[mine], peer)
-        )
-        q_copies[-1].start()
+        remote(query_all.at[mine], query_all.at[mine], q_send, q_recv, peer).start()
+
     def spread(buffer, source, chunk, send_sems, recv_sems, turn):
-        copies = []
-        for n, step in enumerate(FAR_FIRST):
+        for step in FAR_FIRST:
             for kind in (0, 1):
                 axis = kind ^ turn
-                here = me[axis]
-                from_ref = (
-                    buffer.at[chunk, kind, here]
-                    if source is None
-                    else source.at[chunk, kind, lax.rem(here + step, SIDE)]
-                )
-                copies.append(
-                    remote(
-                        from_ref,
-                        buffer.at[chunk, kind, here],
-                        send_sems.at[chunk, kind, n],
-                        recv_sems.at[chunk, kind, here],
-                        along(axis, step),
-                    )
-                )
-                copies[-1].start()
-        return copies
-
-    def arrival(buffer, chunk, kind, there, send_sems, recv_sems):
-        block = buffer.at[chunk, kind, there]
-        remote(
-            block, block, send_sems.at[chunk, kind, 0], recv_sems.at[chunk, kind, there], any_peer
-        ).wait_recv()
-
-    def collect(buffer, chunk, send_sems, recv_sems, turn):
-        for step in FAR_FIRST[::-1]:
-            for kind in (0, 1):
-                there = lax.rem(me[kind ^ turn] + step, SIDE)
-                arrival(buffer, chunk, kind, there, send_sems, recv_sems)
-
-    kv_copies = []
-    for chunk in range(CHUNKS):
-        kv_copies += spread(recv_kv, send_kv, chunk, kv_send, kv_recv, 0)
+                here = kind * SIDE + me[axis]
+                there = kind * SIDE + lax.rem(me[axis] + step, SIDE)
+                remote(
+                    buffer.at[chunk, here] if source is None else source.at[chunk, there],
+                    buffer.at[chunk, here],
+                    send_sems.at[chunk],
+                    recv_sems.at[chunk],
+                    along(axis, step),
+                ).start()
+
+    def spreading(buffer, chunk, send_sems, recv_sems):
+        view = buffer.at[chunk, pl.ds(0, 2 * (SIDE - 1))]
+        return settle(view, send_sems.at[chunk], recv_sems.at[chunk])
+
+    for chunk in range(CHUNKS):
+        spread(recv_kv, send_kv, chunk, kv_send, kv_recv, 0)
 
     load_cache.wait()
     load_new.wait()
@@ -289,11 +272,8 @@
             jnp.logical_and(own_lanes, my_chunk == chunk), own_log, NONE
         )
 
-    for n in range(2 * HALF - 1):
-        came = lax.rem(mine + 1 + n, 2 * HALF)
-        remote(
-            query_all.at[came], query_all.at[came], q_send.at[n], q_recv.at[came], any_peer
-        ).wait_recv()
+    q_all = settle(query_all.at[pl.ds(0, SIDE - 1)], q_send, q_recv)
+    q_all.wait_recv()
 
     span = SIDE * 16
     position_id = lax.broadcasted_iota(jnp.int32, (span, D_HEAD), 0)
@@ -305,7 +285,6 @@
     )
     row16 = lax.broadcasted_iota(jnp.int32, (16, D_HEAD), 0)
     groups = [(kind, j) for kind in (0, 1) for j in range(PAIR)]
-    o_copies = []
     for chunk in range(CHUNKS):
         lengths = jnp.zeros((1, D_HEAD), jnp.int32)
         for n, (kind, j) in enumerate(groups):
@@ -316,9 +295,9 @@
                 slot = (2 * i + 1 - y % 2) * SIDE + y
             lengths = jnp.where(lane_group == n, len_ref[table_smem[0, slot]], lengths)
         valid = positions < lengths
-        collect(recv_kv, chunk, kv_send, kv_recv, 0)
+        spreading(recv_kv, chunk, kv_send, kv_recv).wait_recv()
         every = lax.dot_general(
-            recv_kv[chunk, :, :, :, :, :D_HEAD].reshape(2 * PAIR * span, D_HEAD),
+            recv_kv[chunk, :, :, :, :D_HEAD].reshape(2 * PAIR * span, D_HEAD),
             query_all[chunk * 2 * PAIR : (chunk + 1) * 2 * PAIR].reshape(D_HEAD, D_HEAD),
             (((1,), (1,)), ((), ())),
             preferred_element_type=jnp.float32,
@@ -339,7 +318,9 @@
         outputs = [
             jnp.dot(
                 shares[n * PAD : (n + 1) * PAD],
-                recv_kv[chunk, kind, :, j, :, D_HEAD:].reshape(span, D_HEAD),
+                recv_kv[chunk, kind * SIDE : (kind + 1) * SIDE, j, :, D_HEAD:].reshape(
+                    span, D_HEAD
+                ),
                 preferred_element_type=jnp.float32,
             )[:ROWS]
             for n, (kind, j) in enumerate(groups)
@@ -362,16 +343,18 @@
             jnp.where(row16 == 1, second, jnp.where(row16 == 2, third, 0.0)),
         )
         for kind in (0, 1):
-            pieces[chunk, kind, me[1 - kind]] = jnp.concatenate(
+            pieces[chunk, kind * SIDE + me[1 - kind]] = jnp.concatenate(
                 outputs[kind * PAIR : (kind + 1) * PAIR] + [lines], axis=0
             ).astype(jnp.bfloat16)
-        o_copies += spread(pieces, None, chunk, o_send, o_recv, 1)
-
-    g_copies = []
-    for chunk in range(CHUNKS):
-        collect(pieces, chunk, o_send, o_recv, 1)
+        spread(pieces, None, chunk, o_send, o_recv, 1)
+
+    q_all.wait_send()
+    for chunk in range(CHUNKS):
+        spreading(recv_kv, chunk, kv_send, kv_recv).wait_send()
+    for chunk in range(CHUNKS):
+        spreading(pieces, chunk, o_send, o_recv).wait_recv()
         arrived = [
-            [pieces[chunk, kind, src].astype(jnp.float32) for src in range(SIDE)]
+            [pieces[chunk, kind * SIDE + src].astype(jnp.float32) for src in range(SIDE)]
             for kind in (0, 1)
         ]
         logs = [
@@ -395,23 +378,21 @@
                 acc = term if acc is None else acc + term
             rows.append(acc)
         for kind in (0, 1):
-            gathered[chunk, kind, me[kind]] = jnp.concatenate(
+            gathered[chunk, kind * SIDE + me[kind]] = jnp.concatenate(
                 rows[kind * PAIR : (kind + 1) * PAIR], axis=0
             ).astype(jnp.bfloat16)
-        g_copies += spread(gathered, None, chunk, g_send, g_recv, 0)
+        spread(gathered, None, chunk, g_send, g_recv, 0)
 
     load_weight.wait()
-    s_copies = []
+    for chunk in range(CHUNKS):
+        spreading(pieces, chunk, o_send, o_recv).wait_send()
     per_chunk = n_tracks // CHUNKS
     lane = lax.broadcasted_iota(jnp.int32, (per_chunk, 128), 1)
     for chunk in range(CHUNKS):
-        for step in (0,) + FAR_FIRST[::-1]:
-            for kind in (0, 1):
-                there = lax.rem(me[kind] + step, SIDE)
-                if step:
-                    arrival(gathered, chunk, kind, there, g_send, g_recv)
-                place = ((chunk * 2 + kind) * SIDE + there) * BAND
-                stage[pl.ds(place, BAND), :] = gathered[chunk, kind, there].astype(jnp.float32)
+        spreading(gathered, chunk, g_send, g_recv).wait_recv()
+        stage[pl.ds(chunk * per_chunk * ROWS, per_chunk * ROWS), :] = (
+            gathered[chunk].astype(jnp.float32).reshape(per_chunk * ROWS, D_HEAD)
+        )
         product = None
         for g in range(GROUP):
             left = jnp.concatenate(
@@ -437,29 +418,24 @@
         sums[chunk, head, :, 128:] = jnp.where(lane < 2 * width - 128, middle, last).astype(
             jnp.bfloat16
         )
-        for n, step in enumerate(HEAD_ORDER):
-            s_copies.append(
-                remote(
-                    sums.at[chunk, head],
-                    sums.at[chunk, head],
-                    s_send.at[chunk, n],
-                    s_recv.at[chunk, head],
-                    head_peer(step),
-                )
-            )
-            s_copies[-1].start()
+        for step in HEAD_ORDER:
+            remote(
+                sums.at[chunk, head],
+                sums.at[chunk, head],
+                s_send.at[chunk],
+                s_recv.at[chunk],
+                head_peer(step),
+            ).start()
+    for chunk in range(CHUNKS):
+        spreading(gathered, chunk, g_send, g_recv).wait_send()
+
+    def summing(chunk):
+        view = sums.at[chunk, pl.ds(0, n_heads - 1)]
+        return settle(view, s_send.at[chunk], s_recv.at[chunk])
 
     decoded = None
     for chunk in range(CHUNKS):
-        for step in HEAD_ORDER[::-1]:
-            there = lax.rem(head + step, n_heads)
-            remote(
-                sums.at[chunk, there],
-                sums.at[chunk, there],
-                s_send.at[chunk, 0],
-                s_recv.at[chunk, there],
-                any_peer,
-            ).wait_recv()
+        summing(chunk).wait_recv()
         summed = sums[chunk, 0].astype(jnp.float32)
         for there in range(1, n_heads):
             summed = summed + sums[chunk, there].astype(jnp.float32)
@@ -477,8 +453,8 @@
     for t, rows in enumerate((left, middle, last)):
         out_ref[t * n_tracks : (t + 1) * n_tracks] = rows[:, :width].astype(out_ref.dtype)
 
-    for copy in q_copies + kv_copies + o_copies + g_copies + s_copies:
-        copy.wait_send()
+    for chunk in range(CHUNKS):
+        summing(chunk).wait_send()
 
 
 def shards(queries, new_kv, cache_kv, cache_fill, fresh_kv, fresh_len, owner_slot, out_weight):
@@ -506,26 +482,26 @@
             pltpu.SMEM((1, n_tracks), jnp.int32),
             pltpu.VMEM((PAD, D_HEAD), f32),
             pltpu.VMEM((2 * HALF, PAD, D_HEAD), bf16),
-            pltpu.VMEM((CHUNKS, 2, SIDE, PAIR, depth, 2 * D_HEAD), bf16),
-            pltpu.VMEM((CHUNKS, 2, SIDE, PAIR, depth, 2 * D_HEAD), bf16),
+            pltpu.VMEM((CHUNKS, 2 * SIDE, PAIR, depth, 2 * D_HEAD), bf16),
+            pltpu.VMEM((CHUNKS, 2 * SIDE, PAIR, depth, 2 * D_HEAD), bf16),
             pltpu.VMEM((PAD, D_HEAD), f32),
             pltpu.VMEM((8, D_HEAD), f32),
-            pltpu.VMEM((CHUNKS, 2, SIDE, PIECE, D_HEAD), bf16),
-            pltpu.VMEM((CHUNKS, 2, SIDE, BAND, D_HEAD), bf16),
+            pltpu.VMEM((CHUNKS, 2 * SIDE, PIECE, D_HEAD), bf16),
+            pltpu.VMEM((CHUNKS, 2 * SIDE, BAND, D_HEAD), bf16),
             pltpu.VMEM((n_tracks * ROWS, D_HEAD), f32),
             pltpu.VMEM((CHUNKS, 8, n_tracks // CHUNKS, 256), bf16),
             pltpu.VMEM((n_tracks, n_tracks), bf16),
             dma((8,)),
-            dma((SIDE - 1,)),
-            dma((2 * HALF,)),
-            dma((CHUNKS, 2, SIDE - 1)),
-            dma((CHUNKS, 2, SIDE)),
-            dma((CHUNKS, 2, SIDE - 1)),
-            dma((CHUNKS, 2, SIDE)),
-            dma((CHUNKS, 2, SIDE - 1)),
-            dma((CHUNKS, 2, SIDE)),
-            dma((CHUNKS, 7)),
-            dma((CHUNKS, 8)),
+            dma,
+            dma,
+            dma((CHUNKS,)),
+            dma((CHUNKS,)),
+            dma((CHUNKS,)),
+            dma((CHUNKS,)),
+            dma((CHUNKS,)),
+            dma((CHUNKS,)),
+            dma((CHUNKS,)),
+            dma((CHUNKS,)),
         ],
         compiler_params=pltpu.CompilerParams(
             collective_id=0, has_side_effects=True, vmem_limit_bytes=32 * 1024 * 1024

time: 45.7 us -> 43.7 us (0.956)
  Pallas kernels: 44.3 us -> 42.2 us
    pallas_call x1, Pallas kernels: 44.3 us -> 42.2 us  [shards(): pl.pallas_call(kernel, name='handoff_decode', out_shape=pltpu.VMEM((n_tra...]
where the time goes in v5:
time: 43.7 us; the launch traced here: 43.5 us
  Pallas kernels  42.2 us (97%)
  between operations  0.66 us (2%)
  local copies, waits for them, and re-layouts  0.62 us (1%)
    pallas_call x1, Pallas kernels, shards(): pl.pallas_call(kernel, name='handoff_decode', out_shape=pltpu.VMEM((n_tra...  42.2 us

profile of v5, /device:TPU:1, one launch (start us, length us, event | category | flops | bytes accessed | tf_op | source)
XLA Modules:
  0.0 43.5 jit_solution(1230999080954797825)
XLA Ops:
  0.7 42.2 %handoff_decode.1 = bf16[192,80]{1,0:T(8,128)(2,1)S(1)} custom-call(s32[1]{0:T(128)S(6)} %copy.11.fill_ref, s32[1,64]{1,0:T(1,128)} %bitcast.9, s32[64]{0:T(128)} %len_hbm.1, bf16[1,3,1024]{2,1,0:T(4,128)(2,1)} %query_hbm.1, bf16[1,3,256]{2,1,0:T(4,128)(2,1)} %new_hbm.1, bf16[2048,256]{1,0:T(8,128)(2,1)} %bitcast.7, bf16[64,16,256]{2,1,0:T(8,128)(2,1)} %fresh_hbm.1, ...), custom_call_target="tpu_custom_call" | custom-call | tf_op jit(solution)/shard_map/handoff_decode/pallas_call | solution.py:467
  42.9 0.6 %copy.10 = bf16[64,3,80]{2,0,1:T(8,128)(2,1)} copy(bf16[64,3,80]{2,0,1:T(8,128)(2,1)S(1)} %bitcast.6) | data formatting | bytes 61440

commit v6 on v5

--- a/solution.py
+++ b/solution.py
@@ -15,10 +15,10 @@
 CBLK = 512
 SIDE = 8
 HALF = 4
+PIECE = PAD
 PAIR = 2
-CHUNKS = HALF // PAIR
+ROUNDS = HALF // PAIR
 BAND = PAIR * ROWS
-PIECE = BAND + 16
 NONE = -1e30
 SCALE = D_HEAD**-0.5
 FAR_FIRST = (4, 3, 5, 2, 6, 1, 7)
@@ -107,11 +107,14 @@
     n_heads = 8
     me = (z, y)
 
-    def at(zz, yy):
-        return {"stream": lax.rem(zz, SIDE) * SIDE + lax.rem(yy, SIDE)}
+    place = [[lax.rem(me[axis] + step, SIDE) for step in range(SIDE)] for axis in (0, 1)]
+    device = [
+        [place[0][step] * SIDE + y for step in range(SIDE)],
+        [z * SIDE + place[1][step] for step in range(SIDE)],
+    ]
 
     def along(axis, step):
-        return at(z + step, y) if axis == 0 else at(z, y + step)
+        return {"stream": device[axis][step]}
 
     def head_peer(step):
         return {"head": lax.rem(head + step, n_heads)}
@@ -171,8 +174,7 @@
         ]
     parity = (z + y) % 2
     my_index = jnp.where(parity == 0, y // 2, z // 2)
-    my_chunk, my_group = my_index // PAIR, parity * PAIR + my_index % PAIR
-    mine = my_chunk * 2 * PAIR + my_group
+    mine = my_index * 2 + parity
     my_query = query_f32[...].astype(jnp.bfloat16)
     query_all[mine] = my_query
     width = weight_hbm.shape[0]
@@ -181,21 +183,19 @@
     load_table.wait()
     load_fresh.wait()
 
-    def slot_at(kind, place, i):
+    def slot_at(kind, p, i):
         if kind == 0:
-            return place * SIDE + 2 * i + place % 2
-        return (2 * i + 1 - place % 2) * SIDE + place
-
-    for chunk in range(CHUNKS):
+            return p * SIDE + 2 * i + p % 2
+        return (2 * i + 1 - p % 2) * SIDE + p
+
+    for i in range(HALF):
         for kind in (0, 1):
-            for place in range(SIDE):
-                for j in range(PAIR):
-                    slot = slot_at(kind, place, chunk * PAIR + j)
-                    send_kv[chunk, kind * SIDE + place, j] = fresh[table_smem[0, slot]]
-    for chunk in range(CHUNKS):
+            for p in range(SIDE):
+                send_kv[i, kind * SIDE + p] = fresh[table_smem[0, slot_at(kind, p, i)]]
+    for i in range(HALF):
         for kind in (0, 1):
             here = kind * SIDE + me[kind]
-            recv_kv[chunk, here] = send_kv[chunk, here]
+            recv_kv[i, here] = send_kv[i, here]
 
     pl.semaphore_wait(barrier, len(peers))
 
@@ -203,7 +203,7 @@
         return remote(view, view, send_sem, recv_sem, any_peer)
 
     for step in FAR_FIRST:
-        peer = at(z + step * parity, y + step * (1 - parity))
+        peer = {"stream": jnp.where(parity == 0, device[1][step], device[0][step])}
         remote(query_all.at[mine], query_all.at[mine], q_send, q_recv, peer).start()
 
     def spread(buffer, source, chunk, send_sems, recv_sems, turn):
@@ -211,7 +211,7 @@
             for kind in (0, 1):
                 axis = kind ^ turn
                 here = kind * SIDE + me[axis]
-                there = kind * SIDE + lax.rem(me[axis] + step, SIDE)
+                there = kind * SIDE + place[axis][step]
                 remote(
                     buffer.at[chunk, here] if source is None else source.at[chunk, there],
                     buffer.at[chunk, here],
@@ -224,8 +224,8 @@
         view = buffer.at[chunk, pl.ds(0, 2 * (SIDE - 1))]
         return settle(view, send_sems.at[chunk], recv_sems.at[chunk])
 
-    for chunk in range(CHUNKS):
-        spread(recv_kv, send_kv, chunk, kv_send, kv_recv, 0)
+    for i in range(HALF):
+        spread(recv_kv, send_kv, i, kv_send, kv_recv, 0)
 
     load_cache.wait()
     load_new.wait()
@@ -261,15 +261,15 @@
     top, total, output = merge(parts)
     row_id = lax.broadcasted_iota(jnp.int32, (PAD, D_HEAD), 0)
     lane_id = lax.broadcasted_iota(jnp.int32, (PAD, D_HEAD), 1)
-    own_lane = lane_id == row_id + my_group * PAD
+    own_lane = lane_id == row_id + parity * PAD
     cache_out[...] = output / total
     own_log = jnp.sum(
         jnp.where(own_lane, top + jnp.log(total), 0.0), axis=0, keepdims=True
     )
-    own_lanes = lane_id[:1] // PAD == my_group
-    for chunk in range(CHUNKS):
-        cache_log[chunk : chunk + 1] = jnp.where(
-            jnp.logical_and(own_lanes, my_chunk == chunk), own_log, NONE
+    own_lanes = lane_id[:1] // PAD == parity
+    for i in range(HALF):
+        cache_log[i : i + 1] = jnp.where(
+            jnp.logical_and(own_lanes, my_index == i), own_log, NONE
         )
 
     q_all = settle(query_all.at[pl.ds(0, SIDE - 1)], q_send, q_recv)
@@ -277,36 +277,28 @@
 
     span = SIDE * 16
     position_id = lax.broadcasted_iota(jnp.int32, (span, D_HEAD), 0)
-    lane_group = lax.broadcasted_iota(jnp.int32, (1, D_HEAD), 1) // PAD
+    lane_kind = lax.broadcasted_iota(jnp.int32, (1, D_HEAD), 1) // PAD % 2
     positions = jnp.where(
-        lane_group < PAIR,
+        lane_kind == 0,
         (position_id // 16) * span + y * 16 + position_id % 16,
         z * span + position_id,
     )
-    row16 = lax.broadcasted_iota(jnp.int32, (16, D_HEAD), 0)
-    groups = [(kind, j) for kind in (0, 1) for j in range(PAIR)]
-    for chunk in range(CHUNKS):
-        lengths = jnp.zeros((1, D_HEAD), jnp.int32)
-        for n, (kind, j) in enumerate(groups):
-            i = chunk * PAIR + j
-            if kind == 0:
-                slot = z * SIDE + 2 * i + z % 2
-            else:
-                slot = (2 * i + 1 - y % 2) * SIDE + y
-            lengths = jnp.where(lane_group == n, len_ref[table_smem[0, slot]], lengths)
-        valid = positions < lengths
-        spreading(recv_kv, chunk, kv_send, kv_recv).wait_recv()
+    row8 = lax.broadcasted_iota(jnp.int32, (8, D_HEAD), 0)
+    for i in range(HALF):
+        slots = (z * SIDE + 2 * i + z % 2, (2 * i + 1 - y % 2) * SIDE + y)
+        lengths = [len_ref[table_smem[0, slot]] for slot in slots]
+        valid = positions < jnp.where(lane_kind == 0, lengths[0], lengths[1])
+        pair = query_all[2 * i : 2 * i + 2].reshape(2 * PAD, D_HEAD)
+        queries = jnp.concatenate([pair, pair], axis=0)
+        spreading(recv_kv, i, kv_send, kv_recv).wait_recv()
         every = lax.dot_general(
-            recv_kv[chunk, :, :, :, :D_HEAD].reshape(2 * PAIR * span, D_HEAD),
-            query_all[chunk * 2 * PAIR : (chunk + 1) * 2 * PAIR].reshape(D_HEAD, D_HEAD),
+            recv_kv[i, :, :, :D_HEAD].reshape(2 * span, D_HEAD),
+            queries,
             (((1,), (1,)), ((), ())),
             preferred_element_type=jnp.float32,
-        ).reshape(2, SIDE, PAIR, 16, D_HEAD)
-        scores = every[0, :, 0]
-        for n, (kind, j) in enumerate(groups[1:]):
-            scores = jnp.where(lane_group[None] == n + 1, every[kind, :, j], scores)
-        scores = scores.reshape(span, D_HEAD) * SCALE
-        own = cache_log[chunk : chunk + 1]
+        )
+        scores = jnp.where(lane_kind == 0, every[:span], every[span:]) * SCALE
+        own = cache_log[i : i + 1]
         top = jnp.maximum(
             jnp.max(jnp.where(valid, scores, NONE), axis=0, keepdims=True), own
         )
@@ -317,78 +309,76 @@
         shares = (weights * share).T.astype(jnp.bfloat16)
         outputs = [
             jnp.dot(
-                shares[n * PAD : (n + 1) * PAD],
-                recv_kv[chunk, kind * SIDE : (kind + 1) * SIDE, j, :, D_HEAD:].reshape(
-                    span, D_HEAD
-                ),
+                shares[kind * PAD : (kind + 1) * PAD],
+                recv_kv[i, kind * SIDE : (kind + 1) * SIDE, :, D_HEAD:].reshape(span, D_HEAD),
                 preferred_element_type=jnp.float32,
             )[:ROWS]
-            for n, (kind, j) in enumerate(groups)
+            for kind in (0, 1)
         ]
         own_column = jnp.sum(
             jnp.where(own_lane, own_weight * share, 0.0), axis=1, keepdims=True
         )
         own_part = (own_column * cache_out[...])[:ROWS]
-        outputs = [
-            output + jnp.where(mine == chunk * 2 * PAIR + n, own_part, 0.0)
-            for n, output in enumerate(outputs)
-        ]
         line = top + jnp.log(total)
         first = line.astype(jnp.bfloat16).astype(jnp.float32)
         second = (line - first).astype(jnp.bfloat16).astype(jnp.float32)
         third = line - first - second
         lines = jnp.where(
-            row16 == 0,
+            row8 == 0,
             first,
-            jnp.where(row16 == 1, second, jnp.where(row16 == 2, third, 0.0)),
+            jnp.where(row8 == 1, second, jnp.where(row8 == 2, third, 0.0)),
         )
         for kind in (0, 1):
-            pieces[chunk, kind * SIDE + me[1 - kind]] = jnp.concatenate(
-                outputs[kind * PAIR : (kind + 1) * PAIR] + [lines], axis=0
+            output = outputs[kind] + jnp.where(mine == 2 * i + kind, own_part, 0.0)
+            pieces[i, kind * SIDE + me[1 - kind]] = jnp.concatenate(
+                [output, lines], axis=0
             ).astype(jnp.bfloat16)
-        spread(pieces, None, chunk, o_send, o_recv, 1)
+        spread(pieces, None, i, o_send, o_recv, 1)
 
     q_all.wait_send()
-    for chunk in range(CHUNKS):
-        spreading(recv_kv, chunk, kv_send, kv_recv).wait_send()
-    for chunk in range(CHUNKS):
-        spreading(pieces, chunk, o_send, o_recv).wait_recv()
+    for i in range(HALF):
+        spreading(recv_kv, i, kv_send, kv_recv).wait_send()
+    done = []
+    for i in range(HALF):
+        spreading(pieces, i, o_send, o_recv).wait_recv()
         arrived = [
-            [pieces[chunk, kind * SIDE + src].astype(jnp.float32) for src in range(SIDE)]
+            [pieces[i, kind * SIDE + src].astype(jnp.float32) for src in range(SIDE)]
             for kind in (0, 1)
         ]
         logs = [
-            jnp.concatenate([jnp.sum(a[BAND:], axis=0, keepdims=True) for a in some], axis=0)
+            jnp.concatenate([jnp.sum(a[ROWS:], axis=0, keepdims=True) for a in some], axis=0)
             for some in arrived
         ]
-        logs = jnp.where(lane_group < PAIR, logs[0], logs[1])
+        logs = jnp.where(lane_kind == 0, logs[0], logs[1])
         weights = jnp.exp(logs - jnp.max(logs, axis=0, keepdims=True))
         weights = weights / jnp.sum(weights, axis=0, keepdims=True)
         columns = jnp.concatenate(
             [weights, jnp.zeros((D_HEAD - SIDE, D_HEAD), jnp.float32)], axis=0
         ).T
-        rows = []
-        for n, (kind, j) in enumerate(groups):
+        for kind in (0, 1):
             acc = None
             for src in range(SIDE):
                 term = (
-                    columns[n * PAD : n * PAD + ROWS, src : src + 1]
-                    * arrived[kind][src][j * ROWS : (j + 1) * ROWS]
+                    columns[kind * PAD : kind * PAD + ROWS, src : src + 1]
+                    * arrived[kind][src][:ROWS]
                 )
                 acc = term if acc is None else acc + term
-            rows.append(acc)
-        for kind in (0, 1):
-            gathered[chunk, kind * SIDE + me[kind]] = jnp.concatenate(
-                rows[kind * PAIR : (kind + 1) * PAIR], axis=0
-            ).astype(jnp.bfloat16)
-        spread(gathered, None, chunk, g_send, g_recv, 0)
+            done.append(acc)
+        if len(done) == 2 * PAIR:
+            turn = i // PAIR
+            for kind in (0, 1):
+                gathered[turn, kind * SIDE + me[kind]] = jnp.concatenate(
+                    done[kind::2], axis=0
+                ).astype(jnp.bfloat16)
+            spread(gathered, None, turn, g_send, g_recv, 0)
+            done = []
 
     load_weight.wait()
-    for chunk in range(CHUNKS):
-        spreading(pieces, chunk, o_send, o_recv).wait_send()
-    per_chunk = n_tracks // CHUNKS
+    for i in range(HALF):
+        spreading(pieces, i, o_send, o_recv).wait_send()
+    per_chunk = n_tracks // ROUNDS
     lane = lax.broadcasted_iota(jnp.int32, (per_chunk, 128), 1)
-    for chunk in range(CHUNKS):
+    for chunk in range(ROUNDS):
         spreading(gathered, chunk, g_send, g_recv).wait_recv()
         stage[pl.ds(chunk * per_chunk * ROWS, per_chunk * ROWS), :] = (
             gathered[chunk].astype(jnp.float32).reshape(per_chunk * ROWS, D_HEAD)
@@ -426,7 +416,7 @@
                 s_recv.at[chunk],
                 head_peer(step),
             ).start()
-    for chunk in range(CHUNKS):
+    for chunk in range(ROUNDS):
         spreading(gathered, chunk, g_send, g_recv).wait_send()
 
     def summing(chunk):
@@ -434,7 +424,7 @@
         return settle(view, s_send.at[chunk], s_recv.at[chunk])
 
     decoded = None
-    for chunk in range(CHUNKS):
+    for chunk in range(ROUNDS):
         summing(chunk).wait_recv()
         summed = sums[chunk, 0].astype(jnp.float32)
         for there in range(1, n_heads):
@@ -453,7 +443,7 @@
     for t, rows in enumerate((left, middle, last)):
         out_ref[t * n_tracks : (t + 1) * n_tracks] = rows[:, :width].astype(out_ref.dtype)
 
-    for chunk in range(CHUNKS):
+    for chunk in range(ROUNDS):
         summing(chunk).wait_send()
 
 
@@ -482,26 +472,26 @@
             pltpu.SMEM((1, n_tracks), jnp.int32),
             pltpu.VMEM((PAD, D_HEAD), f32),
             pltpu.VMEM((2 * HALF, PAD, D_HEAD), bf16),
-            pltpu.VMEM((CHUNKS, 2 * SIDE, PAIR, depth, 2 * D_HEAD), bf16),
-            pltpu.VMEM((CHUNKS, 2 * SIDE, PAIR, depth, 2 * D_HEAD), bf16),
+            pltpu.VMEM((HALF, 2 * SIDE, depth, 2 * D_HEAD), bf16),
+            pltpu.VMEM((HALF, 2 * SIDE, depth, 2 * D_HEAD), bf16),
             pltpu.VMEM((PAD, D_HEAD), f32),
             pltpu.VMEM((8, D_HEAD), f32),
-            pltpu.VMEM((CHUNKS, 2 * SIDE, PIECE, D_HEAD), bf16),
-            pltpu.VMEM((CHUNKS, 2 * SIDE, BAND, D_HEAD), bf16),
+            pltpu.VMEM((HALF, 2 * SIDE, PIECE, D_HEAD), bf16),
+            pltpu.VMEM((ROUNDS, 2 * SIDE, BAND, D_HEAD), bf16),
             pltpu.VMEM((n_tracks * ROWS, D_HEAD), f32),
-            pltpu.VMEM((CHUNKS, 8, n_tracks // CHUNKS, 256), bf16),
+            pltpu.VMEM((ROUNDS, 8, n_tracks // ROUNDS, 256), bf16),
             pltpu.VMEM((n_tracks, n_tracks), bf16),
             dma((8,)),
             dma,
             dma,
-            dma((CHUNKS,)),
-            dma((CHUNKS,)),
-            dma((CHUNKS,)),
-            dma((CHUNKS,)),
-            dma((CHUNKS,)),
-            dma((CHUNKS,)),
-            dma((CHUNKS,)),
-            dma((CHUNKS,)),
+            dma((HALF,)),
+            dma((HALF,)),
+            dma((HALF,)),
+            dma((HALF,)),
+            dma((ROUNDS,)),
+            dma((ROUNDS,)),
+            dma((ROUNDS,)),
+            dma((ROUNDS,)),
         ],
         compiler_params=pltpu.CompilerParams(
             collective_id=0, has_side_effects=True, vmem_limit_bytes=32 * 1024 * 1024

time: 43.7 us -> 43.1 us (0.986)
  Pallas kernels: 42.2 us -> 41.7 us
    pallas_call x1, Pallas kernels: 42.2 us -> 41.7 us  [shards(): pl.pallas_call(kernel, name='handoff_decode', out_shape=pltpu.VMEM((n_tra...]
where the time goes in v6:
time: 43.1 us; the launch traced here: 42.9 us
  Pallas kernels  41.7 us (97%)
  between operations  0.66 us (2%)
  local copies, waits for them, and re-layouts  0.62 us (1%)
    pallas_call x1, Pallas kernels, shards(): pl.pallas_call(kernel, name='handoff_decode', out_shape=pltpu.VMEM((n_tra...  41.7 us

profile of v6, /device:TPU:1, one launch (start us, length us, event | category | flops | bytes accessed | tf_op | source)
XLA Modules:
  0.0 42.9 jit_solution(14742613399567500704)
XLA Ops:
  0.7 41.7 %handoff_decode.1 = bf16[192,80]{1,0:T(8,128)(2,1)S(1)} custom-call(s32[1]{0:T(128)S(6)} %copy.11.fill_ref, s32[1,64]{1,0:T(1,128)} %bitcast.9, s32[64]{0:T(128)} %len_hbm.1, bf16[1,3,1024]{2,1,0:T(4,128)(2,1)} %query_hbm.1, bf16[1,3,256]{2,1,0:T(4,128)(2,1)} %new_hbm.1, bf16[2048,256]{1,0:T(8,128)(2,1)} %bitcast.7, bf16[64,16,256]{2,1,0:T(8,128)(2,1)} %fresh_hbm.1, ...), custom_call_target="tpu_custom_call" | custom-call | tf_op jit(solution)/shard_map/handoff_decode/pallas_call | solution.py:457
  42.3 0.6 %copy.10 = bf16[64,3,80]{2,0,1:T(8,128)(2,1)} copy(bf16[64,3,80]{2,0,1:T(8,128)(2,1)S(1)} %bitcast.6) | data formatting | bytes 61440

commit v7 on v6

--- a/solution.py
+++ b/solution.py
@@ -176,7 +176,7 @@
     my_index = jnp.where(parity == 0, y // 2, z // 2)
     mine = my_index * 2 + parity
     my_query = query_f32[...].astype(jnp.bfloat16)
-    query_all[mine] = my_query
+    query_all[mine] = query_f32[:ROWS].astype(jnp.bfloat16)
     width = weight_hbm.shape[0]
     weight[width:] = jnp.zeros((weight.shape[0] - width, weight.shape[1]), weight.dtype)
 
@@ -288,8 +288,13 @@
         slots = (z * SIDE + 2 * i + z % 2, (2 * i + 1 - y % 2) * SIDE + y)
         lengths = [len_ref[table_smem[0, slot]] for slot in slots]
         valid = positions < jnp.where(lane_kind == 0, lengths[0], lengths[1])
-        pair = query_all[2 * i : 2 * i + 2].reshape(2 * PAD, D_HEAD)
-        queries = jnp.concatenate([pair, pair], axis=0)
+        blank = jnp.zeros((PAD - ROWS, D_HEAD), jnp.float32)
+        queries = jnp.concatenate(
+            [query_all[2 * i].astype(jnp.float32), blank]
+            + [query_all[2 * i + 1].astype(jnp.float32), blank],
+            axis=0,
+        )
+        queries = jnp.concatenate([queries, queries], axis=0).astype(jnp.bfloat16)
         spreading(recv_kv, i, kv_send, kv_recv).wait_recv()
         every = lax.dot_general(
             recv_kv[i, :, :, :D_HEAD].reshape(2 * span, D_HEAD),
@@ -471,7 +476,7 @@
             pltpu.VMEM((1, n_tracks), jnp.int32),
             pltpu.SMEM((1, n_tracks), jnp.int32),
             pltpu.VMEM((PAD, D_HEAD), f32),
-            pltpu.VMEM((2 * HALF, PAD, D_HEAD), bf16),
+            pltpu.VMEM((2 * HALF, ROWS, D_HEAD), bf16),
             pltpu.VMEM((HALF, 2 * SIDE, depth, 2 * D_HEAD), bf16),
             pltpu.VMEM((HALF, 2 * SIDE, depth, 2 * D_HEAD), bf16),
             pltpu.VMEM((PAD, D_HEAD), f32),

time: 43.1 us -> 42.9 us (level)
  no operation moved by 1% of the time
where the time goes in v7:
time: 42.9 us; the launch traced here: 42.8 us
  Pallas kernels  41.5 us (97%)
  between operations  0.66 us (2%)
  local copies, waits for them, and re-layouts  0.62 us (1%)
    pallas_call x1, Pallas kernels, shards(): pl.pallas_call(kernel, name='handoff_decode', out_shape=pltpu.VMEM((n_tra...  41.5 us

profile of v7, /device:TPU:1, one launch (start us, length us, event | category | flops | bytes accessed | tf_op | source)
XLA Modules:
  0.0 42.8 jit_solution(7223312383890424058)
XLA Ops:
  0.7 41.5 %handoff_decode.1 = bf16[192,80]{1,0:T(8,128)(2,1)S(1)} custom-call(s32[1]{0:T(128)S(6)} %copy.11.fill_ref, s32[1,64]{1,0:T(1,128)} %bitcast.9, s32[64]{0:T(128)} %len_hbm.1, bf16[1,3,1024]{2,1,0:T(4,128)(2,1)} %query_hbm.1, bf16[1,3,256]{2,1,0:T(4,128)(2,1)} %new_hbm.1, bf16[2048,256]{1,0:T(8,128)(2,1)} %bitcast.7, bf16[64,16,256]{2,1,0:T(8,128)(2,1)} %fresh_hbm.1, ...), custom_call_target="tpu_custom_call" | custom-call | tf_op jit(solution)/shard_map/handoff_decode/pallas_call | solution.py:462
  42.2 0.6 %copy.10 = bf16[64,3,80]{2,0,1:T(8,128)(2,1)} copy(bf16[64,3,80]{2,0,1:T(8,128)(2,1)S(1)} %bitcast.6) | data formatting | bytes 61440

commit v8 on v6

--- a/solution.py
+++ b/solution.py
@@ -478,7 +478,7 @@
             pltpu.VMEM((8, D_HEAD), f32),
             pltpu.VMEM((HALF, 2 * SIDE, PIECE, D_HEAD), bf16),
             pltpu.VMEM((ROUNDS, 2 * SIDE, BAND, D_HEAD), bf16),
-            pltpu.VMEM((n_tracks * ROWS, D_HEAD), f32),
+            pltpu.VMEM(((n_tracks + 1) * ROWS, D_HEAD), f32),
             pltpu.VMEM((ROUNDS, 8, n_tracks // ROUNDS, 256), bf16),
             pltpu.VMEM((n_tracks, n_tracks), bf16),
             dma((8,)),

time: 43.1 us -> 43.1 us (level)
  no operation moved by 1% of the time
where the time goes in v8:
time: 43.1 us; the launch traced here: 42.9 us
  Pallas kernels  41.7 us (97%)
  between operations  0.66 us (2%)
  local copies, waits for them, and re-layouts  0.62 us (1%)
    pallas_call x1, Pallas kernels, shards(): pl.pallas_call(kernel, name='handoff_decode', out_shape=pltpu.VMEM((n_tra...  41.7 us

profile of v8, /device:TPU:1, one launch (start us, length us, event | category | flops | bytes accessed | tf_op | source)
XLA Modules:
  0.0 42.9 jit_solution(3800068553712826040)
XLA Ops:
  0.7 41.7 %handoff_decode.1 = bf16[192,80]{1,0:T(8,128)(2,1)S(1)} custom-call(s32[1]{0:T(128)S(6)} %copy.11.fill_ref, s32[1,64]{1,0:T(1,128)} %bitcast.9, s32[64]{0:T(128)} %len_hbm.1, bf16[1,3,1024]{2,1,0:T(4,128)(2,1)} %query_hbm.1, bf16[1,3,256]{2,1,0:T(4,128)(2,1)} %new_hbm.1, bf16[2048,256]{1,0:T(8,128)(2,1)} %bitcast.7, bf16[64,16,256]{2,1,0:T(8,128)(2,1)} %fresh_hbm.1, ...), custom_call_target="tpu_custom_call" | custom-call | tf_op jit(solution)/shard_map/handoff_decode/pallas_call | solution.py:457
  42.3 0.6 %copy.10 = bf16[64,3,80]{2,0,1:T(8,128)(2,1)} copy(bf16[64,3,80]{2,0,1:T(8,128)(2,1)S(1)} %bitcast.6) | data formatting | bytes 61440

commit v9 on v8

--- a/solution.py
+++ b/solution.py
@@ -162,8 +162,11 @@
     table[...] = track_row
     load_table = pltpu.make_async_copy(table, table_smem, local_sem.at[7])
     load_table.start()
-    picked = slot_of == place_row
-    pick[...] = picked.astype(jnp.float32).T.astype(jnp.bfloat16)
+    per_chunk = n_tracks // ROUNDS
+    term_of = lax.broadcasted_iota(jnp.int32, (n_heads * per_chunk, n_tracks), 0) % per_chunk
+    for chunk in range(ROUNDS):
+        picked = term_of + chunk * per_chunk == place_row
+        pick[chunk] = picked.astype(jnp.float32).T.astype(jnp.bfloat16)
 
     query_f32[...] = jnp.zeros_like(query_f32)
     load_query.wait()
@@ -376,7 +379,6 @@
     load_weight.wait()
     for i in range(HALF):
         spreading(pieces, i, o_send, o_recv).wait_send()
-    per_chunk = n_tracks // ROUNDS
     lane = lax.broadcasted_iota(jnp.int32, (per_chunk, 128), 1)
     for chunk in range(ROUNDS):
         spreading(gathered, chunk, g_send, g_recv).wait_recv()
@@ -426,12 +428,9 @@
     decoded = None
     for chunk in range(ROUNDS):
         summing(chunk).wait_recv()
-        summed = sums[chunk, 0].astype(jnp.float32)
-        for there in range(1, n_heads):
-            summed = summed + sums[chunk, there].astype(jnp.float32)
         term = jnp.dot(
-            pick[:, chunk * per_chunk : (chunk + 1) * per_chunk],
-            summed.astype(jnp.bfloat16),
+            pick[chunk],
+            sums[chunk].reshape(n_heads * per_chunk, sums.shape[3]),
             preferred_element_type=jnp.float32,
         )
         decoded = term if decoded is None else decoded + term
@@ -480,7 +479,7 @@
             pltpu.VMEM((ROUNDS, 2 * SIDE, BAND, D_HEAD), bf16),
             pltpu.VMEM(((n_tracks + 1) * ROWS, D_HEAD), f32),
             pltpu.VMEM((ROUNDS, 8, n_tracks // ROUNDS, 256), bf16),
-            pltpu.VMEM((n_tracks, n_tracks), bf16),
+            pltpu.VMEM((ROUNDS, n_tracks, 8 * n_tracks // ROUNDS), bf16),
             dma((8,)),
             dma,
             dma,

time: 43.1 us -> 43.1 us (level)
  no operation moved by 1% of the time
where the time goes in v9:
time: 43.1 us; the launch traced here: 42.9 us
  Pallas kernels  41.6 us (97%)
  between operations  0.66 us (2%)
  local copies, waits for them, and re-layouts  0.62 us (1%)
    pallas_call x1, Pallas kernels, shards(): pl.pallas_call(kernel, name='handoff_decode', out_shape=pltpu.VMEM((n_tra...  41.6 us

profile of v9, /device:TPU:1, one launch (start us, length us, event | category | flops | bytes accessed | tf_op | source)
XLA Modules:
  0.0 42.9 jit_solution(8758680388710787321)
XLA Ops:
  0.7 41.6 %handoff_decode.1 = bf16[192,80]{1,0:T(8,128)(2,1)S(1)} custom-call(s32[1]{0:T(128)S(6)} %copy.11.fill_ref, s32[1,64]{1,0:T(1,128)} %bitcast.9, s32[64]{0:T(128)} %len_hbm.1, bf16[1,3,1024]{2,1,0:T(4,128)(2,1)} %query_hbm.1, bf16[1,3,256]{2,1,0:T(4,128)(2,1)} %new_hbm.1, bf16[2048,256]{1,0:T(8,128)(2,1)} %bitcast.7, bf16[64,16,256]{2,1,0:T(8,128)(2,1)} %fresh_hbm.1, ...), custom_call_target="tpu_custom_call" | custom-call | tf_op jit(solution)/shard_map/handoff_decode/pallas_call | solution.py:456
  42.3 0.6 %copy.10 = bf16[64,3,80]{2,0,1:T(8,128)(2,1)} copy(bf16[64,3,80]{2,0,1:T(8,128)(2,1)S(1)} %bitcast.6) | data formatting | bytes 61440

commit v10 on v8

--- a/solution.py
+++ b/solution.py
@@ -206,9 +206,9 @@
         peer = {"stream": jnp.where(parity == 0, device[1][step], device[0][step])}
         remote(query_all.at[mine], query_all.at[mine], q_send, q_recv, peer).start()
 
-    def spread(buffer, source, chunk, send_sems, recv_sems, turn):
+    def spread(buffer, source, chunk, send_sems, recv_sems, turn, kinds=(0, 1)):
         for step in FAR_FIRST:
-            for kind in (0, 1):
+            for kind in kinds:
                 axis = kind ^ turn
                 here = kind * SIDE + me[axis]
                 there = kind * SIDE + place[axis][step]
@@ -307,14 +307,6 @@
         total = jnp.sum(weights, axis=0, keepdims=True) + own_weight
         share = 1.0 / total
         shares = (weights * share).T.astype(jnp.bfloat16)
-        outputs = [
-            jnp.dot(
-                shares[kind * PAD : (kind + 1) * PAD],
-                recv_kv[i, kind * SIDE : (kind + 1) * SIDE, :, D_HEAD:].reshape(span, D_HEAD),
-                preferred_element_type=jnp.float32,
-            )[:ROWS]
-            for kind in (0, 1)
-        ]
         own_column = jnp.sum(
             jnp.where(own_lane, own_weight * share, 0.0), axis=1, keepdims=True
         )
@@ -329,11 +321,15 @@
             jnp.where(row8 == 1, second, jnp.where(row8 == 2, third, 0.0)),
         )
         for kind in (0, 1):
-            output = outputs[kind] + jnp.where(mine == 2 * i + kind, own_part, 0.0)
+            output = jnp.dot(
+                shares[kind * PAD : (kind + 1) * PAD],
+                recv_kv[i, kind * SIDE : (kind + 1) * SIDE, :, D_HEAD:].reshape(span, D_HEAD),
+                preferred_element_type=jnp.float32,
+            )[:ROWS] + jnp.where(mine == 2 * i + kind, own_part, 0.0)
             pieces[i, kind * SIDE + me[1 - kind]] = jnp.concatenate(
                 [output, lines], axis=0
             ).astype(jnp.bfloat16)
-        spread(pieces, None, i, o_send, o_recv, 1)
+            spread(pieces, None, i, o_send, o_recv, 1, (kind,))
 
     q_all.wait_send()
     for i in range(HALF):

time: 43.1 us -> 43 us (level)
  no operation moved by 1% of the time
where the time goes in v10:
time: 43 us; the launch traced here: 42.9 us
  Pallas kernels  41.6 us (97%)
  between operations  0.66 us (2%)
  local copies, waits for them, and re-layouts  0.62 us (1%)
    pallas_call x1, Pallas kernels, shards(): pl.pallas_call(kernel, name='handoff_decode', out_shape=pltpu.VMEM((n_tra...  41.6 us

profile of v10, /device:TPU:1, one launch (start us, length us, event | category | flops | bytes accessed | tf_op | source)
XLA Modules:
  0.0 42.9 jit_solution(7720629764938902047)
XLA Ops:
  0.7 41.6 %handoff_decode.1 = bf16[192,80]{1,0:T(8,128)(2,1)S(1)} custom-call(s32[1]{0:T(128)S(6)} %copy.11.fill_ref, s32[1,64]{1,0:T(1,128)} %bitcast.9, s32[64]{0:T(128)} %len_hbm.1, bf16[1,3,1024]{2,1,0:T(4,128)(2,1)} %query_hbm.1, bf16[1,3,256]{2,1,0:T(4,128)(2,1)} %new_hbm.1, bf16[2048,256]{1,0:T(8,128)(2,1)} %bitcast.7, bf16[64,16,256]{2,1,0:T(8,128)(2,1)} %fresh_hbm.1, ...), custom_call_target="tpu_custom_call" | custom-call | tf_op jit(solution)/shard_map/handoff_decode/pallas_call | solution.py:453
  42.2 0.6 %copy.10 = bf16[64,3,80]{2,0,1:T(8,128)(2,1)} copy(bf16[64,3,80]{2,0,1:T(8,128)(2,1)S(1)} %bitcast.6) | data formatting | bytes 61440
